TPU v7x, 256 devices: a whole 4x4x8 slice. The times are simulated.
256 devices in a mesh: tx: 8 (over z), ty: 32 (over x, y, core).
Axes of the slice: x: 4, y: 4, z: 8, core: 2. Of those that a mesh axis runs over, the one named last changes fastest.
Arguments:
- source: bfloat16 [512, 2048, 2, 128], P('tx', 'ty'), may hold values from -6 to 6
- guess: bfloat16 [512, 2048, 2, 128], P('tx', 'ty'), may hold values from -6 to 6
- coefficient: float32 [512, 2048], P('tx', 'ty'), may hold values from 0.25 to 2.5
- leaf_map: float32 [8, 32, 2, 256, 256], P('tx', 'ty'), may hold values from -0.9 to 0.9, as said below
- body_map: bfloat16 [8, 32, 2, 256, 4096], P('tx', 'ty'), may hold values from -0.013671875 to 0.013671875
Outputs:
- top_map: float32 [8, 32, 2, 64, 768], P('tx', 'ty')
- top_outgoing: float32 [8, 32, 2, 64, 128], P('tx', 'ty')
Inputs may be any that keep to these rules, and one draw needn't show every extreme that they name: `leaf_map`: as a complex matrix, each tile's map has spectral norm at most 0.9.
All inputs are finite; a program needn't handle non-finite values.
Results may differ from a plain program's by a relative error of at most 0.0029.
Values may be sent and summed in bfloat16 or wider, within the bound.
No kernel may reach another device: no remote copies, remote signals or barrier semaphores. Data moves between devices by JAX's collectives and lax.ppermute only.
A program may use at most 64 MiB of HBM per device.

v0:
```python
import jax
import jax.numpy as jnp
from jax import lax
from jax.experimental import pallas as pl
from jax.experimental.pallas import tpu as pltpu
from jax.sharding import PartitionSpec as P

F32 = jnp.float32
B16 = jnp.bfloat16
SQUARINGS = 8
SEG = 64
RHS = 128
WIRE = B16
VMEM_LIMIT = 24 * 1024 * 1024


def roles():
    row = lax.axis_index("tx")
    col = lax.axis_index("ty")
    even = (row & 1) == 0
    left = (col & 1) == 0
    inner = (((row + 1) >> 1) & 1) == 1
    upper = ((row >> 1) & 1) == 1
    return even, left, inner, upper


def side_order(even, left):
    return (
        jnp.where(even, 2, 0),
        jnp.where(left, 1, 3),
        jnp.where(even, 0, 2),
        jnp.where(left, 3, 1),
    )


def low_half(shape):
    return lax.broadcasted_iota(jnp.int32, shape, len(shape) - 1) % 128 < SEG


def half_roll(value):
    return jnp.concatenate([value[:, SEG:], value[:, :SEG]], axis=1)


def split(value):
    high = value.astype(B16)
    return high, (value - high.astype(F32)).astype(B16)


def times_i(stacked):
    half = stacked.shape[0] // 2
    return jnp.concatenate([-stacked[half:], stacked[:half]], axis=0)


def embed(stacked):
    return jnp.concatenate([stacked, times_i(stacked)], axis=1)


def dot(left, right):
    return jnp.dot(left, right, preferred_element_type=F32)


def dot_split(left, right):
    return dot(left[0], right[0]) + (dot(left[0], right[1]) + dot(left[1], right[0]))


def complex_dot(left, right):
    lefts = split(left)
    return dot_split((embed(lefts[0]), embed(lefts[1])), split(right))


def neumann(power):
    size = power.shape[1]
    rows = lax.broadcasted_iota(jnp.int32, power.shape, 0)
    cols = lax.broadcasted_iota(jnp.int32, power.shape, 1)
    total = power + jnp.where(rows == cols, 1.0, 0.0).astype(F32)
    power = complex_dot(power, power)
    for k in range(1, SQUARINGS):
        both = total
        if k + 1 < SQUARINGS:
            both = jnp.concatenate([power, total], axis=1)
        if k < 4:
            step = complex_dot(power, both)
        else:
            step = dot(embed(power.astype(B16)), both.astype(B16))
        if k + 1 < SQUARINGS:
            power = step[:, :size]
            step = step[:, size:]
        total = total + step
    return total


def stack(ref, begin, length):
    return jnp.concatenate([ref[0, begin : begin + length], ref[1, begin : begin + length]], axis=0).astype(F32)


def store_stacked(ref, value, begin=0):
    half = value.shape[0] // 2
    ref[0, begin : begin + half] = value[:half].astype(ref.dtype)
    ref[1, begin : begin + half] = value[half:].astype(ref.dtype)


def rows_of(stacked, begin, length):
    half = stacked.shape[0] // 2
    return jnp.concatenate(
        [stacked[begin : begin + length], stacked[half + begin : half + begin + length]], axis=0
    )


def join_rows(parts):
    halves = [p.shape[0] // 2 for p in parts]
    return jnp.concatenate(
        [p[:h] for p, h in zip(parts, halves)] + [p[h:] for p, h in zip(parts, halves)], axis=0
    )


def front_kernel(guess_ref, leaf_ref, row_i, row_k, col_j, col_l, own_ref, send_ref, leaf, sems):
    even, left, inner, _ = roles()
    row = jnp.where(even, SEG - 1, 0)
    col = jnp.where(left, SEG - 1, 0)
    copies = [
        pltpu.make_async_copy(guess_ref.at[row], row_i, sems.at[0]),
        pltpu.make_async_copy(guess_ref.at[SEG - 1 - row], row_k, sems.at[1]),
        pltpu.make_async_copy(guess_ref.at[:, col], col_j, sems.at[2]),
        pltpu.make_async_copy(guess_ref.at[:, SEG - 1 - col], col_l, sems.at[3]),
        pltpu.make_async_copy(leaf_ref, leaf, sems.at[4]),
    ]
    for copy in copies:
        copy.start()
    copies[4].wait()
    low = low_half((SEG, 128))
    crossed = (low & even) | (~low & ~left)
    for part in range(2):
        for place, side in enumerate(side_order(even, left)):
            rows = leaf[part, pl.ds(pl.multiple_of(side * SEG, SEG), SEG), :]
            first = rows[:, :128]
            second = rows[:, 128:]
            near = jnp.where(crossed, second, first)
            far = jnp.where(crossed, first, second)
            near = jnp.where(inner, half_roll(near), near)
            own_ref[part, place * SEG : (place + 1) * SEG, :128] = near
            own_ref[part, place * SEG : (place + 1) * SEG, 128:] = far
            if place < 3:
                send_ref[part, place * SEG : (place + 1) * SEG, :128] = near.astype(send_ref.dtype)
                send_ref[part, place * SEG : (place + 1) * SEG, 128:] = far.astype(send_ref.dtype)
    for copy in copies[:4]:
        copy.wait()


def planes_matrix(size=2 * SEG):
    row = lax.broadcasted_iota(jnp.int32, (size, size), 0)
    col = lax.broadcasted_iota(jnp.int32, (size, size), 1)
    return jnp.where(col == 2 * (row % SEG) + row // SEG, 1.0, 0.0).astype(B16)


def stencil_matrix():
    width = 2 * SEG
    row = lax.broadcasted_iota(jnp.int32, (width, width), 0)
    col = lax.broadcasted_iota(jnp.int32, (width, width), 1)
    apart = jnp.abs(col - 2 * (row % SEG) - row // SEG)
    own = jnp.where(apart == 0, 1.0, 0.0).astype(F32)
    beside = jnp.where(apart == 2, 1.0, 0.0).astype(F32)
    ahead = jnp.concatenate([own, beside - 4.0 * own], axis=1)
    value = jnp.concatenate([jnp.zeros_like(own), own], axis=1)
    return jnp.concatenate([ahead, value], axis=0).astype(B16)


BLOCK = 8
BLOCKS = SEG // BLOCK


def stencil_kernel(
    source_ref, guess_ref, coef_ref, body_ref, flat_ref, body_out, source, guess, coef_rows,
    source_sems, guess_sems, body_sems, coef_sem,
):
    width = 2 * SEG
    chunk = BLOCK * width
    span = BLOCK * SEG

    def source_copy(i):
        rows = pl.ds(i * chunk, chunk)
        return pltpu.make_async_copy(source_ref.at[rows], source.at[rows], source_sems.at[i])

    def guess_copy(i):
        rows = pl.ds(i * chunk, chunk)
        return pltpu.make_async_copy(guess_ref.at[rows], guess.at[rows], guess_sems.at[i])

    def body_copy(i):
        rows = pl.ds(i * SEG, SEG)
        return pltpu.make_async_copy(body_ref.at[rows], body_out.at[rows], body_sems.at[i])

    coef_copy = pltpu.make_async_copy(coef_ref, coef_rows, coef_sem)
    coef_copy.start()
    for i in range(BLOCKS):
        guess_copy(i).start()
        source_copy(i).start()
    for i in range(BLOCKS):
        body_copy(i).start()
    table = stencil_matrix()
    planes = planes_matrix()
    coef_copy.wait()
    guess_copy(0).wait()

    def block(i, carry):
        @pl.when(i + 1 < BLOCKS)
        def _():
            guess_copy(i + 1).wait()

        source_copy(i).wait()
        base = i * chunk

        def rows_at(ref, begin):
            return ref[pl.ds(pl.multiple_of(begin, width), width), :]

        below = rows_at(guess, jnp.maximum(base - width, 0))
        above = rows_at(guess, jnp.minimum(base + chunk, SEG * width - width))
        outer = dot(planes, jnp.concatenate([below, above], axis=1))
        values = {
            -1: jnp.where(i == 0, 0.0, outer[:, :RHS]),
            BLOCK: jnp.where(i == BLOCKS - 1, 0.0, outer[:, RHS:]),
        }
        ahead = {}
        for k in range(0, BLOCK, 2):
            pair = [
                jnp.concatenate([rows_at(source, base + r * width), rows_at(guess, base + r * width)], axis=0)
                for r in (k, k + 1)
            ]
            both = dot(table, jnp.concatenate(pair, axis=1))
            for j, r in enumerate((k, k + 1)):
                ahead[r] = both[:width, j * RHS : (j + 1) * RHS]
                values[r] = both[width:, j * RHS : (j + 1) * RHS]
        coef = coef_rows[pl.ds(pl.multiple_of(i * BLOCK, BLOCK), BLOCK), :].T
        for r in range(BLOCK):
            wave = jnp.broadcast_to(coef[:, r : r + 1], (SEG, RHS))
            sums = ahead[r] + (values[r - 1] + values[r + 1])
            real_part = values[r][:SEG]
            imag_part = values[r][SEG:]
            cells = pl.ds(pl.multiple_of(i * span + r * SEG, SEG), SEG)
            flat_ref[cells, :RHS] = sums[:SEG] + wave * (real_part - 0.5 * imag_part)
            flat_ref[cells, RHS:] = sums[SEG:] + wave * (imag_part + 0.5 * real_part)
        return carry

    lax.fori_loop(0, BLOCKS, block, 0)
    for i in range(BLOCKS):
        body_copy(i).wait()


def leaf_kernel(
    flat_ref, body_ref, across_i, across_j, across_k, across_l, own_ref, send_ref, total, west_ref, east_ref
):
    even, left, _, _ = roles()
    at_row = lax.axis_index("tx")
    at_col = lax.axis_index("ty")
    strips = dot(planes_matrix(), jnp.concatenate([across_i[...], across_k[...]], axis=1))
    south = jnp.where(even, strips[:, RHS:], strips[:, :RHS])
    north = jnp.where(even, strips[:, :RHS], strips[:, RHS:])
    south = jnp.where(at_row == 0, 0.0, south)
    north = jnp.where(at_row == lax.axis_size("tx") - 1, 0.0, north)
    near = across_j[...].astype(F32)
    far = across_l[...].astype(F32)
    west_ref[...] = jnp.where(at_col == 0, 0.0, jnp.where(left, far, near))
    east_ref[...] = jnp.where(at_col == lax.axis_size("ty") - 1, 0.0, jnp.where(left, near, far))
    row8 = lax.broadcasted_iota(jnp.int32, (8, RHS), 0)
    span = BLOCK * SEG

    def block(i):
        cells = []
        for r in range(BLOCK):
            parts = []
            for c in range(2):
                rows = pl.ds(pl.multiple_of(i * span + r * SEG, SEG), SEG)
                flat = flat_ref[rows, c * RHS : (c + 1) * RHS]
                if r == 0:
                    flat = flat + jnp.where(i == 0, south[c * SEG : (c + 1) * SEG], 0.0)
                if r == BLOCK - 1:
                    flat = flat + jnp.where(i == BLOCKS - 1, north[c * SEG : (c + 1) * SEG], 0.0)
                at = 2 * (i * BLOCK + r) + c
                begin = flat[:8] + jnp.where(row8 == 0, west_ref[pl.ds(at, 1), :], 0.0)
                end = flat[SEG - 8 :] + jnp.where(row8 == 7, east_ref[pl.ds(at, 1), :], 0.0)
                parts.append(jnp.concatenate([begin, flat[8 : SEG - 8], end], axis=0).astype(B16))
            cells.append(jnp.concatenate(parts, axis=1))
        return dot(body_ref[:, pl.ds(pl.multiple_of(i * span, span), span)], jnp.concatenate(cells, axis=0))

    total[...] = block(0)

    def add(i, carry):
        total[...] += block(i)
        return carry

    lax.fori_loop(1, BLOCKS, add, 0)
    half = total.shape[0] // 2
    real_part = total[:half, :RHS] - total[half:, RHS:]
    imag_part = total[:half, RHS:] + total[half:, :RHS]
    total[:half, :RHS] = real_part
    total[half:, :RHS] = imag_part
    for part in range(2):
        for place, side in enumerate(side_order(even, left)):
            rows = total[pl.ds(pl.multiple_of(part * half + side * SEG, SEG), SEG), :RHS]
            own_ref[part, place * SEG : (place + 1) * SEG] = rows
            if place < 3:
                send_ref[part, place * SEG : (place + 1) * SEG] = rows.astype(send_ref.dtype)


def merge_rows_kernel(own_ref, partner_ref, face_ref, keep_ref, gain_ref):
    _, _, inner, _ = roles()

    def pick(place):
        mine = stack(own_ref, place * SEG, SEG)
        theirs = stack(partner_ref, place * SEG, SEG)
        return jnp.where(inner, mine, theirs), jnp.where(inner, theirs, mine)

    n_i, u_i = pick(0)
    n_j, u_j = pick(1)
    n_k, _ = pick(2)
    out = jnp.where(inner, stack(own_ref, 3 * SEG, SEG), stack(own_ref, 2 * SEG, SEG))
    inner_n = n_i[:, SEG:128]
    inner_u = u_i[:, :SEG]
    inverse = neumann(complex_dot(inner_u, inner_n))
    into_n = jnp.concatenate([complex_dot(inverse, inner_u), -inverse], axis=1)
    rows = lax.broadcasted_iota(jnp.int32, (128, 128), 0)
    cols = lax.broadcasted_iota(jnp.int32, (128, 128), 1)
    unit = jnp.where((rows == cols) & (cols < SEG), 1.0, 0.0).astype(F32)
    into_u = -unit - complex_dot(inner_n, into_n)
    gain_n = complex_dot(join_rows([n_j[:, SEG:128], n_k[:, SEG:128]]), into_n)
    gain_u = complex_dot(u_j[:, :SEG], into_u)
    gain_out = complex_dot(
        jnp.where(inner, out[:, SEG:128], out[:, :SEG]), jnp.where(inner, into_n, into_u)
    )
    gain = join_rows([rows_of(gain_n, 0, SEG), gain_u, rows_of(gain_n, SEG, SEG), gain_out])
    store_stacked(gain_ref, gain)
    zero = jnp.zeros_like(n_j)
    in_n = complex_dot(gain[:, :SEG], n_i) + join_rows([n_j, zero, n_k, jnp.where(inner, out, 0.0)])
    in_u = complex_dot(gain[:, SEG:], u_i) + join_rows([zero, u_j, zero, jnp.where(inner, 0.0, out)])
    joint = jnp.where(low_half((512, 128)), in_n[:, :128], in_u[:, :128])
    merged = jnp.concatenate([joint, in_n[:, 128:], in_u[:, 128:]], axis=1)
    store_stacked(face_ref, rows_of(merged, 0, 128))
    store_stacked(keep_ref, rows_of(merged, 128, 128))


def load_rows_kernel(own_ref, partner_ref, gain_ref, face_ref, keep_ref):
    _, _, inner, _ = roles()

    def pick(place):
        mine = stack(own_ref, place * SEG, SEG)
        theirs = stack(partner_ref, place * SEG, SEG)
        return jnp.where(inner, mine, theirs), jnp.where(inner, theirs, mine)

    n_i, u_i = pick(0)
    n_j, u_j = pick(1)
    n_k, _ = pick(2)
    out = jnp.where(inner, stack(own_ref, 3 * SEG, SEG), stack(own_ref, 2 * SEG, SEG))
    merged = complex_dot(stack(gain_ref, 0, 256), join_rows([n_i, u_i])) + join_rows([n_j, u_j, n_k, out])
    store_stacked(face_ref, rows_of(merged, 0, 128))
    store_stacked(keep_ref, rows_of(merged, 128, 128))


def merge_cols_kernel(own_ref, across_ref, keep_ref, face_ref, send_ref, out_ref, gain_ref):
    _, left, _, upper = roles()
    own = stack(own_ref, 0, 128)
    across = stack(across_ref, 0, 128)
    keep = stack(keep_ref, 0, 128)
    inverse = neumann(complex_dot(across[:, :128], own[:, :128]))
    bounced = complex_dot(across[:, :128], own[:, 128:])
    carried = complex_dot(keep[:, :128], inverse)
    gained = complex_dot(carried, jnp.concatenate([bounced, across], axis=1))
    store_stacked(gain_ref, jnp.concatenate([gained[:, 256:384], -carried], axis=1))
    mine = keep[:, 128:] + gained[:, :256]
    theirs = -gained[:, 384:]
    west = jnp.where(left, mine, theirs)
    east = jnp.where(left, theirs, mine)
    low = low_half((256, 128))
    west_n, west_u = west[:, :128], west[:, 128:]
    east_n, east_u = east[:, :128], east[:, 128:]
    roll_wn, roll_wu, roll_en, roll_eu = [half_roll(v) for v in (west_n, west_u, east_n, east_u)]
    inner_k = jnp.where(low, west_n, roll_en)
    outer_k = jnp.where(low, west_u, roll_eu)
    east_l = jnp.where(upper, jnp.where(low, roll_en, east_u), jnp.where(low, roll_eu, east_n))
    west_l = jnp.where(upper, jnp.where(low, roll_wn, west_u), jnp.where(low, roll_wu, west_n))
    merged = jnp.concatenate([inner_k, outer_k, east_l, west_l], axis=1)
    face = rows_of(merged, 0, SEG)
    store_stacked(face_ref, face)
    store_stacked(send_ref, face)
    store_stacked(out_ref, rows_of(merged, SEG, SEG))


def load_cols_kernel(own_ref, across_ref, keep_ref, gain_ref, face_ref, send_ref, out_ref):
    sides = join_rows([stack(own_ref, 0, 128), stack(across_ref, 0, 128)])
    merged = stack(keep_ref, 0, 128) + complex_dot(stack(gain_ref, 0, 128), sides)
    face = rows_of(merged, 0, SEG)
    store_stacked(face_ref, face)
    store_stacked(send_ref, face)
    store_stacked(out_ref, rows_of(merged, SEG, SEG))


def top_kernel(
    own_ref, mate_ref, far_ref, far_mate_ref, out_ref,
    own_load, mate_load, far_load, far_mate_load, out_load, map_ref, load_ref,
):
    _, left, _, upper = roles()

    def both(mine_ref, theirs_ref):
        mine = stack(mine_ref, 0, SEG)
        theirs = stack(theirs_ref, 0, SEG)
        return join_rows([jnp.where(left, mine, theirs), jnp.where(left, theirs, mine)])

    near = both(own_ref, mate_ref)
    far = both(far_ref, far_mate_ref)
    rows = stack(out_ref, 0, SEG)
    inverse = neumann(complex_dot(far[:, :128], near[:, :128]))
    near_load = both(own_load, mate_load)
    far_load_rows = both(far_load, far_mate_load)
    bounced = complex_dot(far[:, :128], jnp.concatenate([near[:, 128:], near_load], axis=1))
    carried = complex_dot(rows[:, :128], inverse)
    gained = complex_dot(carried, jnp.concatenate([bounced, far[:, 128:], far_load_rows], axis=1))
    mine = rows[:, 128:] + gained[:, :384]
    theirs = -gained[:, 512:896]
    store_stacked(load_ref, stack(out_load, 0, SEG) + gained[:, 384:512] - gained[:, 896:])
    lower_part = jnp.where(upper, theirs, mine)
    upper_part = jnp.where(upper, mine, theirs)
    store_stacked(
        map_ref,
        jnp.concatenate(
            [lower_part, upper_part[:, 128:256], upper_part[:, :128], upper_part[:, 256:]], axis=1
        ),
    )


def call(kernel, name, outs, *args, kept=0, scratch=()):
    args = [pltpu.with_memory_space_constraint(v, pltpu.HBM) if i < kept else v for i, v in enumerate(args)]
    return pl.pallas_call(
        kernel,
        in_specs=[pl.BlockSpec(memory_space=pltpu.HBM if i < kept else pltpu.VMEM) for i in range(len(args))],
        out_shape=[jax.ShapeDtypeStruct(shape, dtype) for shape, dtype in outs],
        scratch_shapes=list(scratch),
        compiler_params=pltpu.CompilerParams(vmem_limit_bytes=VMEM_LIMIT),
        name=name,
    )(*args)


def swap_near(value, axis):
    return lax.ppermute(value, axis, [(i, i ^ 1) for i in range(lax.axis_size(axis))])


def swap_far(value, axis):
    count = lax.axis_size(axis)
    pairs = []
    for i in range(1, count, 2):
        pairs += [(i, (i + 1) % count), ((i + 1) % count, i)]
    return lax.ppermute(value, axis, pairs)


def from_other_half(value):
    return lax.ppermute(value, "tx", [(i, i ^ 3) for i in range(lax.axis_size("tx"))])


def on_device(source, guess, coefficient, leaf_map, body_map):
    dma = pltpu.SemaphoreType.DMA
    strip = ((SEG, 2, RHS), B16)
    *strips, own, sent = call(
        front_kernel, "front",
        [strip, strip, strip, strip, ((2, 256, 256), F32), ((2, 192, 256), WIRE)],
        guess, leaf_map[0, 0], kept=2, scratch=[pltpu.VMEM((2, 256, 256), F32), dma((5,))],
    )
    row_i, row_k, col_j, col_l = [strip.reshape(128, RHS) for strip in strips]
    across_k = swap_far(row_k, "tx")
    across_l = swap_far(col_l, "ty")
    across_i = swap_near(row_i, "tx")
    across_j = swap_near(col_j, "ty")
    partner = swap_near(sent, "tx")
    flat, body = call(
        stencil_kernel, "stencil",
        [((SEG * SEG, 2 * RHS), F32), ((512, SEG * SEG), B16)],
        source.reshape(SEG * SEG * 2, RHS), guess.reshape(SEG * SEG * 2, RHS), coefficient,
        body_map.reshape(512, SEG * SEG), kept=4,
        scratch=[
            pltpu.VMEM((SEG * SEG * 2, RHS), B16), pltpu.VMEM((SEG * SEG * 2, RHS), B16),
            pltpu.VMEM((SEG, SEG), F32), dma((BLOCKS,)), dma((BLOCKS,)), dma((BLOCKS,)), dma(()),
        ],
    )
    own_load, sent_load = call(
        leaf_kernel, "leaf_loads", [((2, 256, RHS), F32), ((2, 192, RHS), WIRE)],
        flat, body, across_i, across_j, across_k, across_l,
        scratch=[pltpu.VMEM((512, 2 * RHS), F32), pltpu.VMEM((128, RHS), F32), pltpu.VMEM((128, RHS), F32)],
    )
    partner, sent_load = lax.optimization_barrier((partner, sent_load))
    partner_load = swap_near(sent_load, "tx")

    face1, keep1, gain1 = call(
        merge_rows_kernel, "merge_rows",
        [((2, 128, 384), F32), ((2, 128, 384), F32), ((2, 256, 128), F32)], own, partner,
    )
    face1_across = swap_near(face1, "ty")
    face2, send2, out2, gain2 = call(
        merge_cols_kernel, "merge_cols",
        [((2, 64, 512), F32), ((2, 64, 512), WIRE), ((2, 64, 512), F32), ((2, 128, 256), F32)],
        face1, face1_across, keep1,
    )
    face2_far = from_other_half(send2)
    face2_mate = swap_near(face2, "ty")

    load1, keep_load1 = call(
        load_rows_kernel, "load_rows", [((2, 128, RHS), F32)] * 2, own_load, partner_load, gain1
    )
    load1_across = swap_near(load1, "ty")
    load2, send_load2, out_load2 = call(
        load_cols_kernel, "load_cols",
        [((2, 64, RHS), F32), ((2, 64, RHS), WIRE), ((2, 64, RHS), F32)],
        load1, load1_across, keep_load1, gain2,
    )
    load2_far = from_other_half(send_load2)
    load2_mate = swap_near(load2, "ty")
    far_mate = swap_near(face2_far, "ty")
    load_far_mate = swap_near(load2_far, "ty")
    top_map, top_out = call(
        top_kernel, "merge_top", [((2, 64, 768), F32), ((2, 64, RHS), F32)],
        face2, face2_mate, face2_far, far_mate, out2,
        load2, load2_mate, load2_far, load_far_mate, out_load2,
    )
    return top_map[None, None], top_out[None, None]


def solution(mesh):
    placed = (
        P("tx", "ty", None, None),
        P("tx", "ty", None, None),
        P("tx", "ty"),
        P("tx", "ty", None, None, None),
        P("tx", "ty", None, None, None),
    )
    return jax.shard_map(
        on_device,
        mesh=mesh,
        in_specs=placed,
        out_specs=(P("tx", "ty", None, None, None), P("tx", "ty", None, None, None)),
        check_vma=False,
    )
```

profile of v0, /device:TPU:1, one launch (start us, length us, event | category | flops | bytes accessed | tf_op | source)
XLA Modules:
  0.0 52.2 jit_solution(18306502167932104231)
XLA Ops:
  0.6 1.3 %front.1 = (bf16[64,2,128]{2,1,0:T(2,128)(2,1)S(1)}, bf16[64,2,128]{2,1,0:T(2,128)(2,1)S(1)}, bf16[64,2,128]{2,1,0:T(2,128)(2,1)S(1)}, bf16[64,2,128]{2,1,0:T(2,...) custom-call(bf16[64,64,2,128]{3,2,1,0:T(2,128)(2,1)} %guess_ref.1, f32[2,256,256]{2,1,0:T(8,128)} %bitcast.17), custom_call_target="tpu_custom_call" | custom-call | tf_op jit(solution)/shard_map/front/pallas_call | solution.py:429
  2.0 2.6 %collective-permute-start = (bf16[2,192,256]{2,1,0:T(8,128)(2,1)S(1)}, bf16[2,192,256]{2,1,0:T(8,128)(2,1)S(1)}, u32[]{:S(2)}, u32[]{:S(2)}) collective-permute-start(bf16[2,192,256]{2,1,0:T(8,128)(2,1)S(1)} %get-tuple-element.29), channel_id=1, source_target_pairs={{0,32},{32,0},{64,96},{96,64},{128,160},{160,128},{192,224},{224,1... | collective-permute-start | bytes 589832 | tf_op jit(solution)/shard_map/ppermute | solution.py:440
  4.5 0.1 collective-permute-start.1
  4.6 2.7 %collective-permute-start.2 = (bf16[128,128]{1,0:T(8,128)(2,1)S(1)}, bf16[128,128]{1,0:T(8,128)(2,1)S(1)}, u32[]{:S(2)}, u32[]{:S(2)}) collective-permute-start(bf16[128,128]{1,0:T(8,128)(2,1)S(1)} %bitcast.12), channel_id=1, source_target_pairs={{0,1},{1,0},{2,3},{3,2},{4,5},{5,4},{6,7},{7,6},{8,9},{9,8},{10,11... | collective-permute-start | bytes 98312 | tf_op jit(solution)/shard_map/ppermute | solution.py:440
  7.3 3.8 %collective-permute-start.3 = (bf16[128,128]{1,0:T(8,128)(2,1)S(1)}, bf16[128,128]{1,0:T(8,128)(2,1)S(1)}, u32[]{:S(2)}, u32[]{:S(2)}) collective-permute-start(bf16[128,128]{1,0:T(8,128)(2,1)S(1)} %bitcast.11), channel_id=1, source_target_pairs={{32,64},{64,32},{96,128},{128,96},{160,192},{192,160},{224,0},{0,2... | collective-permute-start | bytes 98312 | tf_op jit(solution)/shard_map/ppermute | solution.py:448
  11.2 1.5 %collective-permute-start.4 = (bf16[128,128]{1,0:T(8,128)(2,1)S(1)}, bf16[128,128]{1,0:T(8,128)(2,1)S(1)}, u32[]{:S(2)}, u32[]{:S(2)}) collective-permute-start(bf16[128,128]{1,0:T(8,128)(2,1)S(1)} %bitcast.10), channel_id=1, source_target_pairs={{1,2},{2,1},{3,4},{4,3},{5,6},{6,5},{7,8},{8,7},{9,10},{10,9},{11,... | collective-permute-start | bytes 98312 | tf_op jit(solution)/shard_map/ppermute | solution.py:448
  12.6 6.3 %stencil.1 = (f32[4096,256]{1,0:T(8,128)S(1)}, bf16[512,4096]{1,0:T(8,128)(2,1)S(1)}) custom-call(bf16[8192,128]{1,0:T(8,128)(2,1)} %bitcast.16, bf16[8192,128]{1,0:T(8,128)(2,1)} %bitcast.14, f32[64,64]{1,0:T(8,128)} %coef_ref.1, bf16[512,4096]{1,0:T(8,128)(2,1)} %bitcast.15), custom_call_target="tpu_custom_call" | custom-call | tf_op jit(solution)/shard_map/stencil/pallas_call | solution.py:429
  19.0 0.0 collective-permute-done.1.across_i
  19.0 0.0 collective-permute-done.2.across_j
  19.0 0.0 collective-permute-done.3.across_k
  19.0 0.0 collective-permute-done.4.across_l
  19.0 2.7 %leaf_loads.1 = (f32[2,256,128]{2,1,0:T(8,128)S(1)}, bf16[2,192,128]{2,1,0:T(8,128)(2,1)S(1)}) custom-call(f32[4096,256]{1,0:T(8,128)S(1)} %get-tuple-element.30.flat_ref, bf16[512,4096]{1,0:T(8,128)(2,1)S(1)} %get-tuple-element.31.body_ref, bf16[128,128]{1,0:T(8,128)(2,1)S(1)} %collective-permute-done.1.across_i, ...), custom_call_target="tpu_custom_call" | custom-call | tf_op jit(solution)/shard_map/leaf_loads/pallas_call | solution.py:429
  21.7 0.0 collective-permute-done.partner_ref
  21.7 3.6 %merge_rows.1 = (f32[2,128,384]{2,1,0:T(8,128)S(1)}, f32[2,128,384]{2,1,0:T(8,128)S(1)}, f32[2,256,128]{2,1,0:T(8,128)S(1)}) custom-call(f32[2,256,256]{2,1,0:T(8,128)S(1)} %get-tuple-element.28.own_ref, bf16[2,192,256]{2,1,0:T(8,128)(2,1)S(1)} %collective-permute-done.partner_ref), custom_call_target="tpu_custom_call" | custom-call | tf_op jit(solution)/shard_map/merge_rows/pallas_call | solution.py:429
  25.3 3.9 %collective-permute-start.5 = (f32[2,128,384]{2,1,0:T(8,128)S(1)}, f32[2,128,384]{2,1,0:T(8,128)S(1)}, u32[]{:S(2)}, u32[]{:S(2)}) collective-permute-start(f32[2,128,384]{2,1,0:T(8,128)S(1)} %get-tuple-element.38.own_ref), channel_id=1, source_target_pairs={{0,1},{1,0},{2,3},{3,2},{4,5},{5,4},{6,7},{7,6},{8,9},{9,8},{10,11... | collective-permute-start | bytes 1179656 | tf_op jit(solution)/shard_map/ppermute | solution.py:440
  29.2 0.0 collective-permute-start.9
  29.2 1.3 %collective-permute-done.5.across_ref = f32[2,128,384]{2,1,0:T(8,128)S(1)} collective-permute-done((f32[2,128,384]{2,1,0:T(8,128)S(1)}, f32[2,128,384]{2,1,0:T(8,128)S(1)}, u32[]{:S(2)}, u32[]{:S(2)}) %collective-permute-start.5) | collective-permute-done | bytes 393248 | tf_op jit(solution)/shard_map/ppermute | solution.py:440
  30.6 3.1 %merge_cols.1 = (f32[2,64,512]{2,1,0:T(8,128)S(1)}, bf16[2,64,512]{2,1,0:T(8,128)(2,1)S(1)}, f32[2,64,512]{2,1,0:T(8,128)S(1)}, f32[2,128,256]{2,1,0:T(8,128)S(1)}) custom-call(f32[2,128,384]{2,1,0:T(8,128)S(1)} %get-tuple-element.38.own_ref, f32[2,128,384]{2,1,0:T(8,128)S(1)} %collective-permute-done.5.across_ref, f32[2,128,384]{2,1,0:T(8,128)S(1)} %get-tuple-element.39.keep_ref), custom_call_target="tpu_custom_call" | custom-call | tf_op jit(solution)/shard_map/merge_cols/pallas_call | solution.py:429
  33.7 1.7 %collective-permute-start.7 = (bf16[2,64,512]{2,1,0:T(8,128)(2,1)S(1)}, bf16[2,64,512]{2,1,0:T(8,128)(2,1)S(1)}, u32[]{:S(2)}, u32[]{:S(2)}) collective-permute-start(bf16[2,64,512]{2,1,0:T(8,128)(2,1)S(1)} %get-tuple-element.41), channel_id=1, source_target_pairs={{0,96},{32,64},{64,32},{96,0},{128,224},{160,192},{192,160},{224,1... | collective-permute-start | bytes 393224 | tf_op jit(solution)/shard_map/ppermute | solution.py:452
  35.4 0.7 %collective-permute-start.6 = (f32[2,64,512]{2,1,0:T(8,128)S(1)}, f32[2,64,512]{2,1,0:T(8,128)S(1)}, u32[]{:S(2)}, u32[]{:S(2)}) collective-permute-start(f32[2,64,512]{2,1,0:T(8,128)S(1)} %get-tuple-element.40.own_ref), channel_id=1, source_target_pairs={{0,1},{1,0},{2,3},{3,2},{4,5},{5,4},{6,7},{7,6},{8,9},{9,8},{10,11... | collective-permute-start | bytes 786440 | tf_op jit(solution)/shard_map/ppermute | solution.py:440
  36.0 0.0 collective-permute-done.9.partner_ref
  36.0 0.4 load_rows.1
  36.4 0.1 collective-permute-start.10
  36.5 3.8 %collective-permute-done.7.far_ref = bf16[2,64,512]{2,1,0:T(8,128)(2,1)S(1)} collective-permute-done((bf16[2,64,512]{2,1,0:T(8,128)(2,1)S(1)}, bf16[2,64,512]{2,1,0:T(8,128)(2,1)S(1)}, u32[]{:S(2)}, u32[]{:S(2)}) %collective-permute-start.7) | collective-permute-done | bytes 131104 | tf_op jit(solution)/shard_map/ppermute | solution.py:452
  40.3 1.3 %collective-permute-start.8 = (bf16[2,64,512]{2,1,0:T(8,128)(2,1)S(1)}, bf16[2,64,512]{2,1,0:T(8,128)(2,1)S(1)}, u32[]{:S(2)}, u32[]{:S(2)}) collective-permute-start(bf16[2,64,512]{2,1,0:T(8,128)(2,1)S(1)} %collective-permute-done.7.far_ref), channel_id=1, source_target_pairs={{0,1},{1,0},{2,3},{3,2},{4,5},{5,4},{6,7},{7,6},{8,9},{9,8},{10,11... | collective-permute-start | bytes 393224 | tf_op jit(solution)/shard_map/ppermute | solution.py:440
  41.6 0.0 collective-permute-done.10.across_ref
  41.6 0.4 load_cols.1
  41.9 1.7 %collective-permute-start.12 = (bf16[2,64,128]{2,1,0:T(8,128)(2,1)S(1)}, bf16[2,64,128]{2,1,0:T(8,128)(2,1)S(1)}, u32[]{:S(2)}, u32[]{:S(2)}) collective-permute-start(bf16[2,64,128]{2,1,0:T(8,128)(2,1)S(1)} %get-tuple-element.50), channel_id=1, source_target_pairs={{0,96},{32,64},{64,32},{96,0},{128,224},{160,192},{192,160},{224,1... | collective-permute-start | bytes 98312 | tf_op jit(solution)/shard_map/ppermute | solution.py:452
  43.6 0.3 collective-permute-start.11
  43.9 2.7 %collective-permute-done.12.far_load = bf16[2,64,128]{2,1,0:T(8,128)(2,1)S(1)} collective-permute-done((bf16[2,64,128]{2,1,0:T(8,128)(2,1)S(1)}, bf16[2,64,128]{2,1,0:T(8,128)(2,1)S(1)}, u32[]{:S(2)}, u32[]{:S(2)}) %collective-permute-start.12) | collective-permute-done | bytes 32800 | tf_op jit(solution)/shard_map/ppermute | solution.py:452
  46.6 1.2 %collective-permute-start.13 = (bf16[2,64,128]{2,1,0:T(8,128)(2,1)S(1)}, bf16[2,64,128]{2,1,0:T(8,128)(2,1)S(1)}, u32[]{:S(2)}, u32[]{:S(2)}) collective-permute-start(bf16[2,64,128]{2,1,0:T(8,128)(2,1)S(1)} %collective-permute-done.12.far_load), channel_id=1, source_target_pairs={{0,1},{1,0},{2,3},{3,2},{4,5},{5,4},{6,7},{7,6},{8,9},{9,8},{10,11... | collective-permute-start | bytes 98312 | tf_op jit(solution)/shard_map/ppermute | solution.py:440
  47.7 0.0 collective-permute-done.11.mate_load
  47.8 0.9 %collective-permute-done.13.far_mate_load = bf16[2,64,128]{2,1,0:T(8,128)(2,1)S(1)} collective-permute-done((bf16[2,64,128]{2,1,0:T(8,128)(2,1)S(1)}, bf16[2,64,128]{2,1,0:T(8,128)(2,1)S(1)}, u32[]{:S(2)}, u32[]{:S(2)}) %collective-permute-start.13) | collective-permute-done | bytes 32800 | tf_op jit(solution)/shard_map/ppermute | solution.py:440
  48.6 0.0 collective-permute-done.8.far_mate_ref
  48.6 0.0 collective-permute-done.6.mate_ref
  48.6 3.6 %merge_top.1 = (f32[2,64,768]{2,1,0:T(8,128)}, f32[2,64,128]{2,1,0:T(8,128)}) custom-call(f32[2,64,512]{2,1,0:T(8,128)S(1)} %get-tuple-element.40.own_ref, f32[2,64,512]{2,1,0:T(8,128)S(1)} %collective-permute-done.6.mate_ref, bf16[2,64,512]{2,1,0:T(8,128)(2,1)S(1)} %collective-permute-done.7.far_ref, ...), custom_call_target="tpu_custom_call" | custom-call | tf_op jit(solution)/shard_map/merge_top/pallas_call | solution.py:429
Async XLA Ops:
  2.0 19.7 %collective-permute-start = (bf16[2,192,256]{2,1,0:T(8,128)(2,1)S(1)}, bf16[2,192,256]{2,1,0:T(8,128)(2,1)S(1)}, u32[]{:S(2)}, u32[]{:S(2)}) collective-permute-start(bf16[2,192,256]{2,1,0:T(8,128)(2,1)S(1)} %get-tuple-element.29), channel_id=1, source_target_pairs={{0,32},{32,0},{64,96},{96,64},{128,160},{160,128},{192,224},{224,1... | collective-permute-start | bytes 589832 | tf_op jit(solution)/shard_map/ppermute | solution.py:440
  4.5 14.4 %collective-permute-start.1 = (bf16[128,128]{1,0:T(8,128)(2,1)S(1)}, bf16[128,128]{1,0:T(8,128)(2,1)S(1)}, u32[]{:S(2)}, u32[]{:S(2)}) collective-permute-start(bf16[128,128]{1,0:T(8,128)(2,1)S(1)} %bitcast.13), channel_id=1, source_target_pairs={{0,32},{32,0},{64,96},{96,64},{128,160},{160,128},{192,224},{224,1... | collective-permute-start | bytes 98312 | tf_op jit(solution)/shard_map/ppermute | solution.py:440
  4.6 14.3 %collective-permute-start.2 = (bf16[128,128]{1,0:T(8,128)(2,1)S(1)}, bf16[128,128]{1,0:T(8,128)(2,1)S(1)}, u32[]{:S(2)}, u32[]{:S(2)}) collective-permute-start(bf16[128,128]{1,0:T(8,128)(2,1)S(1)} %bitcast.12), channel_id=1, source_target_pairs={{0,1},{1,0},{2,3},{3,2},{4,5},{5,4},{6,7},{7,6},{8,9},{9,8},{10,11... | collective-permute-start | bytes 98312 | tf_op jit(solution)/shard_map/ppermute | solution.py:440
  7.3 11.7 %collective-permute-start.3 = (bf16[128,128]{1,0:T(8,128)(2,1)S(1)}, bf16[128,128]{1,0:T(8,128)(2,1)S(1)}, u32[]{:S(2)}, u32[]{:S(2)}) collective-permute-start(bf16[128,128]{1,0:T(8,128)(2,1)S(1)} %bitcast.11), channel_id=1, source_target_pairs={{32,64},{64,32},{96,128},{128,96},{160,192},{192,160},{224,0},{0,2... | collective-permute-start | bytes 98312 | tf_op jit(solution)/shard_map/ppermute | solution.py:448
  11.2 7.8 %collective-permute-start.4 = (bf16[128,128]{1,0:T(8,128)(2,1)S(1)}, bf16[128,128]{1,0:T(8,128)(2,1)S(1)}, u32[]{:S(2)}, u32[]{:S(2)}) collective-permute-start(bf16[128,128]{1,0:T(8,128)(2,1)S(1)} %bitcast.10), channel_id=1, source_target_pairs={{1,2},{2,1},{3,4},{4,3},{5,6},{6,5},{7,8},{8,7},{9,10},{10,9},{11,... | collective-permute-start | bytes 98312 | tf_op jit(solution)/shard_map/ppermute | solution.py:448
  25.3 5.3 %collective-permute-start.5 = (f32[2,128,384]{2,1,0:T(8,128)S(1)}, f32[2,128,384]{2,1,0:T(8,128)S(1)}, u32[]{:S(2)}, u32[]{:S(2)}) collective-permute-start(f32[2,128,384]{2,1,0:T(8,128)S(1)} %get-tuple-element.38.own_ref), channel_id=1, source_target_pairs={{0,1},{1,0},{2,3},{3,2},{4,5},{5,4},{6,7},{7,6},{8,9},{9,8},{10,11... | collective-permute-start | bytes 1179656 | tf_op jit(solution)/shard_map/ppermute | solution.py:440
  29.2 6.8 %collective-permute-start.9 = (bf16[2,192,128]{2,1,0:T(8,128)(2,1)S(1)}, bf16[2,192,128]{2,1,0:T(8,128)(2,1)S(1)}, u32[]{:S(2)}, u32[]{:S(2)}) collective-permute-start(bf16[2,192,128]{2,1,0:T(8,128)(2,1)S(1)} %get-tuple-element.44), channel_id=1, source_target_pairs={{0,32},{32,0},{64,96},{96,64},{128,160},{160,128},{192,224},{224,1... | collective-permute-start | bytes 294920 | tf_op jit(solution)/shard_map/ppermute | solution.py:440
  33.7 6.6 %collective-permute-start.7 = (bf16[2,64,512]{2,1,0:T(8,128)(2,1)S(1)}, bf16[2,64,512]{2,1,0:T(8,128)(2,1)S(1)}, u32[]{:S(2)}, u32[]{:S(2)}) collective-permute-start(bf16[2,64,512]{2,1,0:T(8,128)(2,1)S(1)} %get-tuple-element.41), channel_id=1, source_target_pairs={{0,96},{32,64},{64,32},{96,0},{128,224},{160,192},{192,160},{224,1... | collective-permute-start | bytes 393224 | tf_op jit(solution)/shard_map/ppermute | solution.py:452
  35.4 13.2 %collective-permute-start.6 = (f32[2,64,512]{2,1,0:T(8,128)S(1)}, f32[2,64,512]{2,1,0:T(8,128)S(1)}, u32[]{:S(2)}, u32[]{:S(2)}) collective-permute-start(f32[2,64,512]{2,1,0:T(8,128)S(1)} %get-tuple-element.40.own_ref), channel_id=1, source_target_pairs={{0,1},{1,0},{2,3},{3,2},{4,5},{5,4},{6,7},{7,6},{8,9},{9,8},{10,11... | collective-permute-start | bytes 786440 | tf_op jit(solution)/shard_map/ppermute | solution.py:440
  36.4 5.2 %collective-permute-start.10 = (f32[2,128,128]{2,1,0:T(8,128)S(1)}, f32[2,128,128]{2,1,0:T(8,128)S(1)}, u32[]{:S(2)}, u32[]{:S(2)}) collective-permute-start(f32[2,128,128]{2,1,0:T(8,128)S(1)} %get-tuple-element.46.own_ref), channel_id=1, source_target_pairs={{0,1},{1,0},{2,3},{3,2},{4,5},{5,4},{6,7},{7,6},{8,9},{9,8},{10,11... | collective-permute-start | bytes 393224 | tf_op jit(solution)/shard_map/ppermute | solution.py:440
  40.3 8.3 %collective-permute-start.8 = (bf16[2,64,512]{2,1,0:T(8,128)(2,1)S(1)}, bf16[2,64,512]{2,1,0:T(8,128)(2,1)S(1)}, u32[]{:S(2)}, u32[]{:S(2)}) collective-permute-start(bf16[2,64,512]{2,1,0:T(8,128)(2,1)S(1)} %collective-permute-done.7.far_ref), channel_id=1, source_target_pairs={{0,1},{1,0},{2,3},{3,2},{4,5},{5,4},{6,7},{7,6},{8,9},{9,8},{10,11... | collective-permute-start | bytes 393224 | tf_op jit(solution)/shard_map/ppermute | solution.py:440
  41.9 4.7 %collective-permute-start.12 = (bf16[2,64,128]{2,1,0:T(8,128)(2,1)S(1)}, bf16[2,64,128]{2,1,0:T(8,128)(2,1)S(1)}, u32[]{:S(2)}, u32[]{:S(2)}) collective-permute-start(bf16[2,64,128]{2,1,0:T(8,128)(2,1)S(1)} %get-tuple-element.50), channel_id=1, source_target_pairs={{0,96},{32,64},{64,32},{96,0},{128,224},{160,192},{192,160},{224,1... | collective-permute-start | bytes 98312 | tf_op jit(solution)/shard_map/ppermute | solution.py:452
  43.6 4.1 %collective-permute-start.11 = (f32[2,64,128]{2,1,0:T(8,128)S(1)}, f32[2,64,128]{2,1,0:T(8,128)S(1)}, u32[]{:S(2)}, u32[]{:S(2)}) collective-permute-start(f32[2,64,128]{2,1,0:T(8,128)S(1)} %get-tuple-element.49.own_load), channel_id=1, source_target_pairs={{0,1},{1,0},{2,3},{3,2},{4,5},{5,4},{6,7},{7,6},{8,9},{9,8},{10,11... | collective-permute-start | bytes 196616 | tf_op jit(solution)/shard_map/ppermute | solution.py:440
  46.6 2.0 %collective-permute-start.13 = (bf16[2,64,128]{2,1,0:T(8,128)(2,1)S(1)}, bf16[2,64,128]{2,1,0:T(8,128)(2,1)S(1)}, u32[]{:S(2)}, u32[]{:S(2)}) collective-permute-start(bf16[2,64,128]{2,1,0:T(8,128)(2,1)S(1)} %collective-permute-done.12.far_load), channel_id=1, source_target_pairs={{0,1},{1,0},{2,3},{3,2},{4,5},{5,4},{6,7},{7,6},{8,9},{9,8},{10,11... | collective-permute-start | bytes 98312 | tf_op jit(solution)/shard_map/ppermute | solution.py:440
where the time goes:
time: 52.3 us; the launch traced here: 52.2 us
  Pallas kernels  21.4 us (41%)
  starting transfers between devices  21.4 us (41%)
  waiting for transfers between devices  8.69 us (17%)
  between operations  0.74 us (1%)
    pallas_call x8, Pallas kernels, call(): pl.pallas_call(kernel, in_specs=[pl.BlockSpec(memory_space=pltpu.HBM if i...  21.4 us
    ppermute x10, starting transfers between devices, swap_near(): lax.ppermute(value, axis, [(i, i ^ 1) for i in range(lax.axis_size(axis))])  12.7 us
    ppermute x2, waiting for transfers between devices, from_other_half(): lax.ppermute(value, 'tx', [(i, i ^ 3) for i in range(lax.axis_size('tx'))])  6.46 us
    ppermute x2, starting transfers between devices, swap_far(): return lax.ppermute(value, axis, pairs)  5.3 us
    ppermute x2, starting transfers between devices, from_other_half(): lax.ppermute(value, 'tx', [(i, i ^ 3) for i in range(lax.axis_size('tx'))])  3.4 us
    ppermute x10, waiting for transfers between devices, swap_near(): lax.ppermute(value, axis, [(i, i ^ 1) for i in range(lax.axis_size(axis))])  2.22 us
  transfers between devices with their start and end apart: 14, of which 4 were waited for; matrix products, arithmetic and copies ran while one was open for 0% of the time, Pallas kernels for 25%

commit v1 on v0

--- a/solution.py
+++ b/solution.py
@@ -66,6 +66,27 @@
 def complex_dot(left, right):
     lefts = split(left)
     return dot_split((embed(lefts[0]), embed(lefts[1])), split(right))
+
+
+def neumann_small(power):
+    power = embed(power)
+    rows = lax.broadcasted_iota(jnp.int32, power.shape, 0)
+    cols = lax.broadcasted_iota(jnp.int32, power.shape, 1)
+    total = power + jnp.where(rows == cols, 1.0, 0.0).astype(F32)
+    parts = split(power)
+    power = dot_split(parts, parts)
+    for k in range(1, SQUARINGS):
+        last = k + 1 == SQUARINGS
+        both = total if last else jnp.concatenate([power, total], axis=1)
+        if k < 3:
+            step = dot_split(split(power), split(both))
+        else:
+            step = dot(power.astype(B16), both.astype(B16))
+        if not last:
+            power = step[:, :128]
+            step = step[:, 128:]
+        total = total + step
+    return total
 
 
 def neumann(power):
@@ -78,7 +99,7 @@
         both = total
         if k + 1 < SQUARINGS:
             both = jnp.concatenate([power, total], axis=1)
-        if k < 4:
+        if k < 3:
             step = complex_dot(power, both)
         else:
             step = dot(embed(power.astype(B16)), both.astype(B16))
@@ -113,12 +134,17 @@
     )
 
 
-def front_kernel(guess_ref, leaf_ref, row_i, row_k, col_j, col_l, own_ref, send_ref, leaf, sems):
+STRIP = 12 * SEG
+
+
+def front_kernel(guess_ref, cells_ref, leaf_ref, row_k, col_j, col_l, own_ref, send_ref, leaf, sems):
     even, left, inner, _ = roles()
     row = jnp.where(even, SEG - 1, 0)
     col = jnp.where(left, SEG - 1, 0)
     copies = [
-        pltpu.make_async_copy(guess_ref.at[row], row_i, sems.at[0]),
+        pltpu.make_async_copy(
+            cells_ref.at[pl.ds(pl.multiple_of(row * 128, 128), 128)], send_ref.at[pl.ds(STRIP, 128)], sems.at[0]
+        ),
         pltpu.make_async_copy(guess_ref.at[SEG - 1 - row], row_k, sems.at[1]),
         pltpu.make_async_copy(guess_ref.at[:, col], col_j, sems.at[2]),
         pltpu.make_async_copy(guess_ref.at[:, SEG - 1 - col], col_l, sems.at[3]),
@@ -140,8 +166,9 @@
             own_ref[part, place * SEG : (place + 1) * SEG, :128] = near
             own_ref[part, place * SEG : (place + 1) * SEG, 128:] = far
             if place < 3:
-                send_ref[part, place * SEG : (place + 1) * SEG, :128] = near.astype(send_ref.dtype)
-                send_ref[part, place * SEG : (place + 1) * SEG, 128:] = far.astype(send_ref.dtype)
+                at = (part * 3 + place) * 2 * SEG
+                send_ref[at : at + SEG] = near.astype(send_ref.dtype)
+                send_ref[at + SEG : at + 2 * SEG] = far.astype(send_ref.dtype)
     for copy in copies[:4]:
         copy.wait()
 
@@ -164,8 +191,10 @@
     return jnp.concatenate([ahead, value], axis=0).astype(B16)
 
 
-BLOCK = 8
+COSTS = (5.0, 3.0, 0.4, 0.8, 3.0)
+BLOCK = 16
 BLOCKS = SEG // BLOCK
+AHEAD = 3
 
 
 def stencil_kernel(
@@ -185,22 +214,27 @@
         return pltpu.make_async_copy(guess_ref.at[rows], guess.at[rows], guess_sems.at[i])
 
     def body_copy(i):
-        rows = pl.ds(i * SEG, SEG)
+        rows = pl.ds(i * (512 // BLOCKS), 512 // BLOCKS)
         return pltpu.make_async_copy(body_ref.at[rows], body_out.at[rows], body_sems.at[i])
 
     coef_copy = pltpu.make_async_copy(coef_ref, coef_rows, coef_sem)
     coef_copy.start()
-    for i in range(BLOCKS):
+    for i in range(AHEAD):
         guess_copy(i).start()
         source_copy(i).start()
-    for i in range(BLOCKS):
-        body_copy(i).start()
     table = stencil_matrix()
     planes = planes_matrix()
     coef_copy.wait()
     guess_copy(0).wait()
 
     def block(i, carry):
+        @pl.when(i + AHEAD < BLOCKS)
+        def _():
+            guess_copy(i + AHEAD).start()
+            source_copy(i + AHEAD).start()
+
+        body_copy(i).start()
+
         @pl.when(i + 1 < BLOCKS)
         def _():
             guess_copy(i + 1).wait()
@@ -219,6 +253,17 @@
             BLOCK: jnp.where(i == BLOCKS - 1, 0.0, outer[:, RHS:]),
         }
         ahead = {}
+        coef = coef_rows[pl.ds(pl.multiple_of(i * BLOCK, BLOCK), BLOCK), :].T
+
+        def finish(r):
+            wave = jnp.broadcast_to(coef[:, r : r + 1], (SEG, RHS))
+            sums = ahead[r] + (values[r - 1] + values[r + 1])
+            real_part = values[r][:SEG]
+            imag_part = values[r][SEG:]
+            cells = pl.ds(pl.multiple_of(i * span + r * SEG, SEG), SEG)
+            flat_ref[cells, :RHS] = sums[:SEG] + wave * (real_part - 0.5 * imag_part)
+            flat_ref[cells, RHS:] = sums[SEG:] + wave * (imag_part + 0.5 * real_part)
+
         for k in range(0, BLOCK, 2):
             pair = [
                 jnp.concatenate([rows_at(source, base + r * width), rows_at(guess, base + r * width)], axis=0)
@@ -228,15 +273,10 @@
             for j, r in enumerate((k, k + 1)):
                 ahead[r] = both[:width, j * RHS : (j + 1) * RHS]
                 values[r] = both[width:, j * RHS : (j + 1) * RHS]
-        coef = coef_rows[pl.ds(pl.multiple_of(i * BLOCK, BLOCK), BLOCK), :].T
-        for r in range(BLOCK):
-            wave = jnp.broadcast_to(coef[:, r : r + 1], (SEG, RHS))
-            sums = ahead[r] + (values[r - 1] + values[r + 1])
-            real_part = values[r][:SEG]
-            imag_part = values[r][SEG:]
-            cells = pl.ds(pl.multiple_of(i * span + r * SEG, SEG), SEG)
-            flat_ref[cells, :RHS] = sums[:SEG] + wave * (real_part - 0.5 * imag_part)
-            flat_ref[cells, RHS:] = sums[SEG:] + wave * (imag_part + 0.5 * real_part)
+            if k > 0:
+                finish(k - 1)
+            finish(k)
+        finish(BLOCK - 1)
         return carry
 
     lax.fori_loop(0, BLOCKS, block, 0)
@@ -245,12 +285,12 @@
 
 
 def leaf_kernel(
-    flat_ref, body_ref, across_i, across_j, across_k, across_l, own_ref, send_ref, total, west_ref, east_ref
+    flat_ref, body_ref, across_j, across_k, across_l, partner_ref, own_ref, send_ref, total, west_ref, east_ref
 ):
     even, left, _, _ = roles()
     at_row = lax.axis_index("tx")
     at_col = lax.axis_index("ty")
-    strips = dot(planes_matrix(), jnp.concatenate([across_i[...], across_k[...]], axis=1))
+    strips = dot(planes_matrix(), jnp.concatenate([partner_ref[STRIP:], across_k[...]], axis=1))
     south = jnp.where(even, strips[:, RHS:], strips[:, :RHS])
     north = jnp.where(even, strips[:, :RHS], strips[:, RHS:])
     south = jnp.where(at_row == 0, 0.0, south)
@@ -303,9 +343,13 @@
 def merge_rows_kernel(own_ref, partner_ref, face_ref, keep_ref, gain_ref):
     _, _, inner, _ = roles()
 
+    def sent(place, part):
+        at = (part * 3 + place) * 2 * SEG
+        return jnp.concatenate([partner_ref[at : at + SEG], partner_ref[at + SEG : at + 2 * SEG]], axis=1)
+
     def pick(place):
         mine = stack(own_ref, place * SEG, SEG)
-        theirs = stack(partner_ref, place * SEG, SEG)
+        theirs = jnp.concatenate([sent(place, 0), sent(place, 1)], axis=0).astype(F32)
         return jnp.where(inner, mine, theirs), jnp.where(inner, theirs, mine)
 
     n_i, u_i = pick(0)
@@ -314,8 +358,9 @@
     out = jnp.where(inner, stack(own_ref, 3 * SEG, SEG), stack(own_ref, 2 * SEG, SEG))
     inner_n = n_i[:, SEG:128]
     inner_u = u_i[:, :SEG]
-    inverse = neumann(complex_dot(inner_u, inner_n))
-    into_n = jnp.concatenate([complex_dot(inverse, inner_u), -inverse], axis=1)
+    solved = neumann_small(complex_dot(inner_u, inner_n))
+    carried = dot_split(split(solved), split(inner_u))
+    into_n = jnp.concatenate([carried, -solved[:, :SEG]], axis=1)
     rows = lax.broadcasted_iota(jnp.int32, (128, 128), 0)
     cols = lax.broadcasted_iota(jnp.int32, (128, 128), 1)
     unit = jnp.where((rows == cols) & (cols < SEG), 1.0, 0.0).astype(F32)
@@ -353,7 +398,7 @@
     store_stacked(keep_ref, rows_of(merged, 128, 128))
 
 
-def merge_cols_kernel(own_ref, across_ref, keep_ref, face_ref, send_ref, out_ref, gain_ref):
+def merge_cols_kernel(own_ref, across_ref, keep_ref, face_ref, send_near, out_ref, gain_ref):
     _, left, _, upper = roles()
     own = stack(own_ref, 0, 128)
     across = stack(across_ref, 0, 128)
@@ -378,44 +423,49 @@
     merged = jnp.concatenate([inner_k, outer_k, east_l, west_l], axis=1)
     face = rows_of(merged, 0, SEG)
     store_stacked(face_ref, face)
-    store_stacked(send_ref, face)
+    store_stacked(send_near, face[:, :128])
     store_stacked(out_ref, rows_of(merged, SEG, SEG))
 
 
-def load_cols_kernel(own_ref, across_ref, keep_ref, gain_ref, face_ref, send_ref, out_ref):
+def load_cols_kernel(own_ref, across_ref, keep_ref, gain_ref, map_ref, out_map, face_ref, send_ref, out_ref):
     sides = join_rows([stack(own_ref, 0, 128), stack(across_ref, 0, 128)])
     merged = stack(keep_ref, 0, 128) + complex_dot(stack(gain_ref, 0, 128), sides)
-    face = rows_of(merged, 0, SEG)
-    store_stacked(face_ref, face)
-    store_stacked(send_ref, face)
-    store_stacked(out_ref, rows_of(merged, SEG, SEG))
-
-
-def top_kernel(
-    own_ref, mate_ref, far_ref, far_mate_ref, out_ref,
-    own_load, mate_load, far_load, far_mate_load, out_load, map_ref, load_ref,
-):
-    _, left, _, upper = roles()
-
-    def both(mine_ref, theirs_ref):
-        mine = stack(mine_ref, 0, SEG)
-        theirs = stack(theirs_ref, 0, SEG)
-        return join_rows([jnp.where(left, mine, theirs), jnp.where(left, theirs, mine)])
-
-    near = both(own_ref, mate_ref)
-    far = both(far_ref, far_mate_ref)
+    for half in range(2):
+        face_ref[half, :, :512] = map_ref[half]
+        face_ref[half, :, 512:] = merged[half * 128 : half * 128 + SEG]
+        send_ref[half, :, :384] = map_ref[half, :, 128:].astype(send_ref.dtype)
+        send_ref[half, :, 384:] = merged[half * 128 : half * 128 + SEG].astype(send_ref.dtype)
+        out_ref[half, :, :512] = out_map[half]
+        out_ref[half, :, 512:] = merged[half * 128 + SEG : half * 128 + 128]
+
+
+def sides_of(mine_ref, theirs_ref):
+    _, left, _, _ = roles()
+    mine = stack(mine_ref, 0, SEG)
+    theirs = stack(theirs_ref, 0, SEG)
+    return join_rows([jnp.where(left, mine, theirs), jnp.where(left, theirs, mine)])
+
+
+def top_solve_kernel(own_ref, mate_ref, far_ref, far_mate_ref, out_ref, carried_ref, mine_ref):
+    near = sides_of(own_ref, mate_ref)
+    far = sides_of(far_ref, far_mate_ref)
     rows = stack(out_ref, 0, SEG)
-    inverse = neumann(complex_dot(far[:, :128], near[:, :128]))
-    near_load = both(own_load, mate_load)
-    far_load_rows = both(far_load, far_mate_load)
-    bounced = complex_dot(far[:, :128], jnp.concatenate([near[:, 128:], near_load], axis=1))
+    inverse = neumann(complex_dot(far, near[:, :128]))
+    bounced = complex_dot(far, near[:, 128:])
     carried = complex_dot(rows[:, :128], inverse)
-    gained = complex_dot(carried, jnp.concatenate([bounced, far[:, 128:], far_load_rows], axis=1))
-    mine = rows[:, 128:] + gained[:, :384]
-    theirs = -gained[:, 512:896]
-    store_stacked(load_ref, stack(out_load, 0, SEG) + gained[:, 384:512] - gained[:, 896:])
-    lower_part = jnp.where(upper, theirs, mine)
-    upper_part = jnp.where(upper, mine, theirs)
+    store_stacked(carried_ref, carried)
+    store_stacked(mine_ref, rows[:, 128:] + complex_dot(carried, bounced))
+
+
+def top_kernel(carried_ref, mine_ref, far_ref, far_mate_ref, map_ref, load_ref):
+    _, _, _, upper = roles()
+    far = sides_of(far_ref, far_mate_ref).astype(B16)
+    mine = stack(mine_ref, 0, SEG)
+    lefts = split(stack(carried_ref, 0, SEG))
+    theirs = -(dot(embed(lefts[0]), far) + dot(embed(lefts[1]), far))
+    store_stacked(load_ref, mine[:, 384:] + theirs[:, 384:])
+    lower_part = jnp.where(upper, theirs[:, :384], mine[:, :384])
+    upper_part = jnp.where(upper, mine[:, :384], theirs[:, :384])
     store_stacked(
         map_ref,
         jnp.concatenate(
@@ -424,7 +474,7 @@
     )
 
 
-def call(kernel, name, outs, *args, kept=0, scratch=()):
+def call(kernel, name, outs, *args, kept=0, scratch=(), cost=1.0):
     args = [pltpu.with_memory_space_constraint(v, pltpu.HBM) if i < kept else v for i, v in enumerate(args)]
     return pl.pallas_call(
         kernel,
@@ -432,6 +482,7 @@
         out_shape=[jax.ShapeDtypeStruct(shape, dtype) for shape, dtype in outs],
         scratch_shapes=list(scratch),
         compiler_params=pltpu.CompilerParams(vmem_limit_bytes=VMEM_LIMIT),
+        cost_estimate=pl.CostEstimate(flops=int(cost * 1.1e9), bytes_accessed=0, transcendentals=0),
         name=name,
     )(*args)
 
@@ -457,20 +508,20 @@
     strip = ((SEG, 2, RHS), B16)
     *strips, own, sent = call(
         front_kernel, "front",
-        [strip, strip, strip, strip, ((2, 256, 256), F32), ((2, 192, 256), WIRE)],
-        guess, leaf_map[0, 0], kept=2, scratch=[pltpu.VMEM((2, 256, 256), F32), dma((5,))],
-    )
-    row_i, row_k, col_j, col_l = [strip.reshape(128, RHS) for strip in strips]
+        [strip, strip, strip, ((2, 256, 256), F32), ((STRIP + 128, 128), WIRE)],
+        guess, guess.reshape(SEG * SEG * 2, RHS), leaf_map[0, 0], kept=3,
+        scratch=[pltpu.VMEM((2, 256, 256), F32), dma((5,))],
+    )
+    row_k, col_j, col_l = [strip.reshape(128, RHS) for strip in strips]
+    partner = swap_near(sent, "tx")
     across_k = swap_far(row_k, "tx")
     across_l = swap_far(col_l, "ty")
-    across_i = swap_near(row_i, "tx")
     across_j = swap_near(col_j, "ty")
-    partner = swap_near(sent, "tx")
     flat, body = call(
         stencil_kernel, "stencil",
         [((SEG * SEG, 2 * RHS), F32), ((512, SEG * SEG), B16)],
         source.reshape(SEG * SEG * 2, RHS), guess.reshape(SEG * SEG * 2, RHS), coefficient,
-        body_map.reshape(512, SEG * SEG), kept=4,
+        body_map.reshape(512, SEG * SEG), kept=4, cost=1.0,
         scratch=[
             pltpu.VMEM((SEG * SEG * 2, RHS), B16), pltpu.VMEM((SEG * SEG * 2, RHS), B16),
             pltpu.VMEM((SEG, SEG), F32), dma((BLOCKS,)), dma((BLOCKS,)), dma((BLOCKS,)), dma(()),
@@ -478,7 +529,7 @@
     )
     own_load, sent_load = call(
         leaf_kernel, "leaf_loads", [((2, 256, RHS), F32), ((2, 192, RHS), WIRE)],
-        flat, body, across_i, across_j, across_k, across_l,
+        flat, body, across_j, across_k, across_l, partner, cost=2.5,
         scratch=[pltpu.VMEM((512, 2 * RHS), F32), pltpu.VMEM((128, RHS), F32), pltpu.VMEM((128, RHS), F32)],
     )
     partner, sent_load = lax.optimization_barrier((partner, sent_load))
@@ -486,34 +537,35 @@
 
     face1, keep1, gain1 = call(
         merge_rows_kernel, "merge_rows",
-        [((2, 128, 384), F32), ((2, 128, 384), F32), ((2, 256, 128), F32)], own, partner,
+        [((2, 128, 384), F32), ((2, 128, 384), F32), ((2, 256, 128), F32)], own, partner, cost=COSTS[4],
     )
     face1_across = swap_near(face1, "ty")
-    face2, send2, out2, gain2 = call(
+    load1, keep_load1 = call(
+        load_rows_kernel, "load_rows", [((2, 128, RHS), F32)] * 2, own_load, partner_load, gain1, cost=COSTS[0]
+    )
+    load1_across = swap_near(load1, "ty")
+    map2, near2, out_map2, gain2 = call(
         merge_cols_kernel, "merge_cols",
-        [((2, 64, 512), F32), ((2, 64, 512), WIRE), ((2, 64, 512), F32), ((2, 128, 256), F32)],
-        face1, face1_across, keep1,
-    )
-    face2_far = from_other_half(send2)
+        [((2, 64, 512), F32), ((2, 64, 128), WIRE), ((2, 64, 512), F32), ((2, 128, 256), F32)],
+        face1, face1_across, keep1, cost=COSTS[1],
+    )
+    far_near = from_other_half(near2)
+    face2, rest2, out2 = call(
+        load_cols_kernel, "load_cols", [((2, 64, 640), F32), ((2, 64, 512), WIRE), ((2, 64, 640), F32)],
+        load1, load1_across, keep_load1, gain2, map2, out_map2, cost=COSTS[2],
+    )
     face2_mate = swap_near(face2, "ty")
-
-    load1, keep_load1 = call(
-        load_rows_kernel, "load_rows", [((2, 128, RHS), F32)] * 2, own_load, partner_load, gain1
-    )
-    load1_across = swap_near(load1, "ty")
-    load2, send_load2, out_load2 = call(
-        load_cols_kernel, "load_cols",
-        [((2, 64, RHS), F32), ((2, 64, RHS), WIRE), ((2, 64, RHS), F32)],
-        load1, load1_across, keep_load1, gain2,
-    )
-    load2_far = from_other_half(send_load2)
-    load2_mate = swap_near(load2, "ty")
-    far_mate = swap_near(face2_far, "ty")
-    load_far_mate = swap_near(load2_far, "ty")
+    far_rest = from_other_half(rest2)
+    far_near_mate = swap_near(far_near, "ty")
+    carried, mine = call(
+        top_solve_kernel, "top_solve", [((2, 64, 128), F32), ((2, 64, 512), F32)],
+        face2, face2_mate, far_near, far_near_mate, out2, cost=COSTS[3],
+    )
+    far_rest, carried = lax.optimization_barrier((far_rest, carried))
+    far_rest_mate = swap_near(far_rest, "ty")
     top_map, top_out = call(
         top_kernel, "merge_top", [((2, 64, 768), F32), ((2, 64, RHS), F32)],
-        face2, face2_mate, face2_far, far_mate, out2,
-        load2, load2_mate, load2_far, load_far_mate, out_load2,
+        carried, mine, far_rest, far_rest_mate,
     )
     return top_map[None, None], top_out[None, None]
 

time: 52.3 us -> 43.3 us (0.83)
  waiting for transfers between devices: 8.69 us -> 3.29 us
  Pallas kernels: 21.4 us -> 18.1 us
    ppermute x2, waiting for transfers between devices: 6.46 us -> 1.41 us  [from_other_half(): lax.ppermute(value, 'tx', [(i, i ^ 3) for i in range(lax.axis_size('tx'))])]
    pallas_call x8 -> x9, Pallas kernels: 21.4 us -> 18.1 us  [call(): pl.pallas_call(kernel, in_specs=[pl.BlockSpec(memory_space=pltpu.HBM if i...]
    ppermute x10 -> x8, starting transfers between devices: 12.7 us -> 11.9 us  [swap_near(): lax.ppermute(value, axis, [(i, i ^ 1) for i in range(lax.axis_size(axis))])]
    ppermute x2, starting transfers between devices: 5.3 us -> 5.85 us  [swap_far(): return lax.ppermute(value, axis, pairs)]
    ppermute x10 -> x8, waiting for transfers between devices: 2.22 us -> 1.87 us  [swap_near(): lax.ppermute(value, axis, [(i, i ^ 1) for i in range(lax.axis_size(axis))])]
  transfers between devices with their start and end apart: 14 -> 12, of which waited for: 4 -> 3; matrix products, arithmetic and copies ran while one was open for 0% -> 0% of each run, Pallas kernels for 25% -> 31%
where the time goes in v1:
time: 43.3 us; the launch traced here: 43.2 us
  starting transfers between devices  21.1 us (49%)
  Pallas kernels  18.1 us (42%)
  waiting for transfers between devices  3.29 us (8%)
  between operations  0.75 us (2%)
    pallas_call x9, Pallas kernels, call(): pl.pallas_call(kernel, in_specs=[pl.BlockSpec(memory_space=pltpu.HBM if i...  18.1 us
    ppermute x8, starting transfers between devices, swap_near(): lax.ppermute(value, axis, [(i, i ^ 1) for i in range(lax.axis_size(axis))])  11.9 us
    ppermute x2, starting transfers between devices, swap_far(): return lax.ppermute(value, axis, pairs)  5.85 us
    ppermute x2, starting transfers between devices, from_other_half(): lax.ppermute(value, 'tx', [(i, i ^ 3) for i in range(lax.axis_size('tx'))])  3.34 us
    ppermute x8, waiting for transfers between devices, swap_near(): lax.ppermute(value, axis, [(i, i ^ 1) for i in range(lax.axis_size(axis))])  1.87 us
    ppermute x2, waiting for transfers between devices, from_other_half(): lax.ppermute(value, 'tx', [(i, i ^ 3) for i in range(lax.axis_size('tx'))])  1.41 us
  transfers between devices with their start and end apart: 12, of which 3 were waited for; matrix products, arithmetic and copies ran while one was open for 0% of the time, Pallas kernels for 31%

profile of v1, /device:TPU:1, one launch (start us, length us, event | category | flops | bytes accessed | tf_op | source)
XLA Modules:
  0.0 43.2 jit_solution(5552332072191915412)
XLA Ops:
  0.6 1.3 %front.1 = (bf16[64,2,128]{2,1,0:T(2,128)(2,1)S(1)}, bf16[64,2,128]{2,1,0:T(2,128)(2,1)S(1)}, bf16[64,2,128]{2,1,0:T(2,128)(2,1)S(1)}, f32[2,256,256]{2,1,0:T(8,128)S(1)}, bf16[896,128]{1,0:T(8,128)(2,1)S(1)}) custom-call(bf16[64,64,2,128]{3,2,1,0:T(2,128)(2,1)} %guess_ref.1, bf16[8192,128]{1,0:T(8,128)(2,1)} %bitcast.12, f32[2,256,256]{2,1,0:T(8,128)} %bitcast.16), custom_call_target="tpu_custom_call" | custom-call | flops 1100000000 | tf_op jit(solution)/shard_map/front/pallas_call | solution.py:479
  2.0 2.6 %collective-permute-start.3 = (bf16[896,128]{1,0:T(8,128)(2,1)S(1)}, bf16[896,128]{1,0:T(8,128)(2,1)S(1)}, u32[]{:S(2)}, u32[]{:S(2)}) collective-permute-start(bf16[896,128]{1,0:T(8,128)(2,1)S(1)} %get-tuple-element.36), channel_id=1, source_target_pairs={{0,32},{32,0},{64,96},{96,64},{128,160},{160,128},{192,224},{224,1... | collective-permute-start | bytes 688136 | tf_op jit(solution)/shard_map/ppermute | solution.py:491
  4.5 4.7 %collective-permute-start.1 = (bf16[128,128]{1,0:T(8,128)(2,1)S(1)}, bf16[128,128]{1,0:T(8,128)(2,1)S(1)}, u32[]{:S(2)}, u32[]{:S(2)}) collective-permute-start(bf16[128,128]{1,0:T(8,128)(2,1)S(1)} %bitcast.11), channel_id=1, source_target_pairs={{32,64},{64,32},{96,128},{128,96},{160,192},{192,160},{224,0},{0,2... | collective-permute-start | bytes 98312 | tf_op jit(solution)/shard_map/ppermute | solution.py:499
  9.2 1.2 %collective-permute-start = (bf16[128,128]{1,0:T(8,128)(2,1)S(1)}, bf16[128,128]{1,0:T(8,128)(2,1)S(1)}, u32[]{:S(2)}, u32[]{:S(2)}) collective-permute-start(bf16[128,128]{1,0:T(8,128)(2,1)S(1)} %bitcast.10), channel_id=1, source_target_pairs={{0,1},{1,0},{2,3},{3,2},{4,5},{5,4},{6,7},{7,6},{8,9},{9,8},{10,11... | collective-permute-start | bytes 98312 | tf_op jit(solution)/shard_map/ppermute | solution.py:491
  10.4 1.2 %collective-permute-start.2 = (bf16[128,128]{1,0:T(8,128)(2,1)S(1)}, bf16[128,128]{1,0:T(8,128)(2,1)S(1)}, u32[]{:S(2)}, u32[]{:S(2)}) collective-permute-start(bf16[128,128]{1,0:T(8,128)(2,1)S(1)} %bitcast.9), channel_id=1, source_target_pairs={{1,2},{2,1},{3,4},{4,3},{5,6},{6,5},{7,8},{8,7},{9,10},{10,9},{11,... | collective-permute-start | bytes 98312 | tf_op jit(solution)/shard_map/ppermute | solution.py:499
  11.6 4.6 %stencil.1 = (f32[4096,256]{1,0:T(8,128)S(1)}, bf16[512,4096]{1,0:T(8,128)(2,1)S(1)}) custom-call(bf16[8192,128]{1,0:T(8,128)(2,1)} %bitcast.15, bf16[8192,128]{1,0:T(8,128)(2,1)} %bitcast.13, f32[64,64]{1,0:T(8,128)} %coef_ref.1, bf16[512,4096]{1,0:T(8,128)(2,1)} %bitcast.14), custom_call_target="tpu_custom_call" | custom-call | flops 1100000000 | tf_op jit(solution)/shard_map/stencil/pallas_call | solution.py:479
  16.2 0.0 collective-permute-done.1.across_k
  16.2 0.0 collective-permute-done.across_j
  16.2 0.0 collective-permute-done.2.across_l
  16.3 0.0 collective-permute-done.3.partner_ref
  16.3 2.0 %leaf_loads.1 = (f32[2,256,128]{2,1,0:T(8,128)S(1)}, bf16[2,192,128]{2,1,0:T(8,128)(2,1)S(1)}) custom-call(f32[4096,256]{1,0:T(8,128)S(1)} %get-tuple-element.31.flat_ref, bf16[512,4096]{1,0:T(8,128)(2,1)S(1)} %get-tuple-element.32.body_ref, bf16[128,128]{1,0:T(8,128)(2,1)S(1)} %collective-permute-done.across_j, ...), custom_call_target="tpu_custom_call" | custom-call | flops 2750000128 | tf_op jit(solution)/shard_map/leaf_loads/pallas_call | solution.py:479
  18.2 0.1 collective-permute-start.4
  18.3 2.8 %merge_rows.1 = (f32[2,128,384]{2,1,0:T(8,128)S(1)}, f32[2,128,384]{2,1,0:T(8,128)S(1)}, f32[2,256,128]{2,1,0:T(8,128)S(1)}) custom-call(f32[2,256,256]{2,1,0:T(8,128)S(1)} %get-tuple-element.40.own_ref, bf16[896,128]{1,0:T(8,128)(2,1)S(1)} %collective-permute-done.3.partner_ref), custom_call_target="tpu_custom_call" | custom-call | flops 3300000000 | tf_op jit(solution)/shard_map/merge_rows/pallas_call | solution.py:479
  21.2 4.2 %collective-permute-start.6 = (f32[2,128,384]{2,1,0:T(8,128)S(1)}, f32[2,128,384]{2,1,0:T(8,128)S(1)}, u32[]{:S(2)}, u32[]{:S(2)}) collective-permute-start(f32[2,128,384]{2,1,0:T(8,128)S(1)} %get-tuple-element.45.own_ref), channel_id=1, source_target_pairs={{0,1},{1,0},{2,3},{3,2},{4,5},{5,4},{6,7},{7,6},{8,9},{9,8},{10,11... | collective-permute-start | bytes 1179656 | tf_op jit(solution)/shard_map/ppermute | solution.py:491
  25.4 0.0 collective-permute-done.4.partner_ref
  25.4 0.4 load_rows.1
  25.8 1.8 %collective-permute-start.5 = (f32[2,128,128]{2,1,0:T(8,128)S(1)}, f32[2,128,128]{2,1,0:T(8,128)S(1)}, u32[]{:S(2)}, u32[]{:S(2)}) collective-permute-start(f32[2,128,128]{2,1,0:T(8,128)S(1)} %get-tuple-element.43.own_ref), channel_id=1, source_target_pairs={{0,1},{1,0},{2,3},{3,2},{4,5},{5,4},{6,7},{7,6},{8,9},{9,8},{10,11... | collective-permute-start | bytes 393224 | tf_op jit(solution)/shard_map/ppermute | solution.py:491
  27.6 0.0 collective-permute-done.6.across_ref
  27.6 3.0 %merge_cols.1 = (f32[2,64,512]{2,1,0:T(8,128)S(1)}, bf16[2,64,128]{2,1,0:T(8,128)(2,1)S(1)}, f32[2,64,512]{2,1,0:T(8,128)S(1)}, f32[2,128,256]{2,1,0:T(8,128)S(1)}) custom-call(f32[2,128,384]{2,1,0:T(8,128)S(1)} %get-tuple-element.45.own_ref, f32[2,128,384]{2,1,0:T(8,128)S(1)} %collective-permute-done.6.across_ref, f32[2,128,384]{2,1,0:T(8,128)S(1)} %get-tuple-element.46.keep_ref), custom_call_target="tpu_custom_call" | custom-call | flops 3300000000 | tf_op jit(solution)/shard_map/merge_cols/pallas_call | solution.py:479
  30.5 0.0 collective-permute-done.5.across_ref
  30.5 0.4 load_cols.1
  30.9 0.1 collective-permute-start.8
  31.0 1.7 %collective-permute-start.9 = (bf16[2,64,128]{2,1,0:T(8,128)(2,1)S(1)}, bf16[2,64,128]{2,1,0:T(8,128)(2,1)S(1)}, u32[]{:S(2)}, u32[]{:S(2)}) collective-permute-start(bf16[2,64,128]{2,1,0:T(8,128)(2,1)S(1)} %get-tuple-element.52), channel_id=1, source_target_pairs={{0,96},{32,64},{64,32},{96,0},{128,224},{160,192},{192,160},{224,1... | collective-permute-start | bytes 98312 | tf_op jit(solution)/shard_map/ppermute | solution.py:503
  32.7 1.6 %collective-permute-start.7 = (bf16[2,64,512]{2,1,0:T(8,128)(2,1)S(1)}, bf16[2,64,512]{2,1,0:T(8,128)(2,1)S(1)}, u32[]{:S(2)}, u32[]{:S(2)}) collective-permute-start(bf16[2,64,512]{2,1,0:T(8,128)(2,1)S(1)} %get-tuple-element.50), channel_id=1, source_target_pairs={{0,96},{32,64},{64,32},{96,0},{128,224},{160,192},{192,160},{224,1... | collective-permute-start | bytes 393224 | tf_op jit(solution)/shard_map/ppermute | solution.py:503
  34.4 1.4 %collective-permute-done.9.far_ref = bf16[2,64,128]{2,1,0:T(8,128)(2,1)S(1)} collective-permute-done((bf16[2,64,128]{2,1,0:T(8,128)(2,1)S(1)}, bf16[2,64,128]{2,1,0:T(8,128)(2,1)S(1)}, u32[]{:S(2)}, u32[]{:S(2)}) %collective-permute-start.9) | collective-permute-done | bytes 32800 | tf_op jit(solution)/shard_map/ppermute | solution.py:503
  35.8 1.5 %collective-permute-start.10 = (bf16[2,64,128]{2,1,0:T(8,128)(2,1)S(1)}, bf16[2,64,128]{2,1,0:T(8,128)(2,1)S(1)}, u32[]{:S(2)}, u32[]{:S(2)}) collective-permute-start(bf16[2,64,128]{2,1,0:T(8,128)(2,1)S(1)} %collective-permute-done.9.far_ref), channel_id=1, source_target_pairs={{0,1},{1,0},{2,3},{3,2},{4,5},{5,4},{6,7},{7,6},{8,9},{9,8},{10,11... | collective-permute-start | bytes 98312 | tf_op jit(solution)/shard_map/ppermute | solution.py:491
  37.3 0.9 %collective-permute-done.10.far_mate_ref = bf16[2,64,128]{2,1,0:T(8,128)(2,1)S(1)} collective-permute-done((bf16[2,64,128]{2,1,0:T(8,128)(2,1)S(1)}, bf16[2,64,128]{2,1,0:T(8,128)(2,1)S(1)}, u32[]{:S(2)}, u32[]{:S(2)}) %collective-permute-start.10) | collective-permute-done | bytes 32800 | tf_op jit(solution)/shard_map/ppermute | solution.py:491
  38.1 0.0 collective-permute-done.8.mate_ref
  38.1 2.6 %top_solve.1 = (f32[2,64,128]{2,1,0:T(8,128)S(1)}, f32[2,64,512]{2,1,0:T(8,128)S(1)}) custom-call(f32[2,64,640]{2,1,0:T(8,128)S(1)} %get-tuple-element.51.own_ref, f32[2,64,640]{2,1,0:T(8,128)S(1)} %collective-permute-done.8.mate_ref, bf16[2,64,128]{2,1,0:T(8,128)(2,1)S(1)} %collective-permute-done.9.far_ref, ...), custom_call_target="tpu_custom_call" | custom-call | flops 880000000 | tf_op jit(solution)/shard_map/top_solve/pallas_call | solution.py:479
  40.7 0.0 collective-permute-done.7.far_ref
  40.7 0.4 %collective-permute-start.11 = (bf16[2,64,512]{2,1,0:T(8,128)(2,1)S(1)}, bf16[2,64,512]{2,1,0:T(8,128)(2,1)S(1)}, u32[]{:S(2)}, u32[]{:S(2)}) collective-permute-start(bf16[2,64,512]{2,1,0:T(8,128)(2,1)S(1)} %collective-permute-done.7.far_ref), channel_id=1, source_target_pairs={{0,1},{1,0},{2,3},{3,2},{4,5},{5,4},{6,7},{7,6},{8,9},{9,8},{10,11... | collective-permute-start | bytes 393224 | tf_op jit(solution)/shard_map/ppermute | solution.py:491
  41.2 1.0 %collective-permute-done.11.far_mate_ref = bf16[2,64,512]{2,1,0:T(8,128)(2,1)S(1)} collective-permute-done((bf16[2,64,512]{2,1,0:T(8,128)(2,1)S(1)}, bf16[2,64,512]{2,1,0:T(8,128)(2,1)S(1)}, u32[]{:S(2)}, u32[]{:S(2)}) %collective-permute-start.11) | collective-permute-done | bytes 131104 | tf_op jit(solution)/shard_map/ppermute | solution.py:491
  42.2 1.0 %merge_top.1 = (f32[2,64,768]{2,1,0:T(8,128)}, f32[2,64,128]{2,1,0:T(8,128)}) custom-call(f32[2,64,128]{2,1,0:T(8,128)S(1)} %get-tuple-element.55.carried_ref, f32[2,64,512]{2,1,0:T(8,128)S(1)} %get-tuple-element.56.mine_ref, bf16[2,64,512]{2,1,0:T(8,128)(2,1)S(1)} %collective-permute-done.7.far_ref, bf16[2,64,512]{2,1,0:T(8,128)(2,1)S(1)} %collective-permute-done.11.far_mate_ref), custom_call_target="tpu_custom_call" | custom-call | flops 1100000000 | tf_op jit(solution)/shard_map/merge_top/pallas_call | solution.py:479
Async XLA Ops:
  2.0 14.3 %collective-permute-start.3 = (bf16[896,128]{1,0:T(8,128)(2,1)S(1)}, bf16[896,128]{1,0:T(8,128)(2,1)S(1)}, u32[]{:S(2)}, u32[]{:S(2)}) collective-permute-start(bf16[896,128]{1,0:T(8,128)(2,1)S(1)} %get-tuple-element.36), channel_id=1, source_target_pairs={{0,32},{32,0},{64,96},{96,64},{128,160},{160,128},{192,224},{224,1... | collective-permute-start | bytes 688136 | tf_op jit(solution)/shard_map/ppermute | solution.py:491
  4.5 11.7 %collective-permute-start.1 = (bf16[128,128]{1,0:T(8,128)(2,1)S(1)}, bf16[128,128]{1,0:T(8,128)(2,1)S(1)}, u32[]{:S(2)}, u32[]{:S(2)}) collective-permute-start(bf16[128,128]{1,0:T(8,128)(2,1)S(1)} %bitcast.11), channel_id=1, source_target_pairs={{32,64},{64,32},{96,128},{128,96},{160,192},{192,160},{224,0},{0,2... | collective-permute-start | bytes 98312 | tf_op jit(solution)/shard_map/ppermute | solution.py:499
  9.2 7.0 %collective-permute-start = (bf16[128,128]{1,0:T(8,128)(2,1)S(1)}, bf16[128,128]{1,0:T(8,128)(2,1)S(1)}, u32[]{:S(2)}, u32[]{:S(2)}) collective-permute-start(bf16[128,128]{1,0:T(8,128)(2,1)S(1)} %bitcast.10), channel_id=1, source_target_pairs={{0,1},{1,0},{2,3},{3,2},{4,5},{5,4},{6,7},{7,6},{8,9},{9,8},{10,11... | collective-permute-start | bytes 98312 | tf_op jit(solution)/shard_map/ppermute | solution.py:491
  10.4 5.8 %collective-permute-start.2 = (bf16[128,128]{1,0:T(8,128)(2,1)S(1)}, bf16[128,128]{1,0:T(8,128)(2,1)S(1)}, u32[]{:S(2)}, u32[]{:S(2)}) collective-permute-start(bf16[128,128]{1,0:T(8,128)(2,1)S(1)} %bitcast.9), channel_id=1, source_target_pairs={{1,2},{2,1},{3,4},{4,3},{5,6},{6,5},{7,8},{8,7},{9,10},{10,9},{11,... | collective-permute-start | bytes 98312 | tf_op jit(solution)/shard_map/ppermute | solution.py:499
  18.2 7.2 %collective-permute-start.4 = (bf16[2,192,128]{2,1,0:T(8,128)(2,1)S(1)}, bf16[2,192,128]{2,1,0:T(8,128)(2,1)S(1)}, u32[]{:S(2)}, u32[]{:S(2)}) collective-permute-start(bf16[2,192,128]{2,1,0:T(8,128)(2,1)S(1)} %get-tuple-element.39), channel_id=1, source_target_pairs={{0,32},{32,0},{64,96},{96,64},{128,160},{160,128},{192,224},{224,1... | collective-permute-start | bytes 294920 | tf_op jit(solution)/shard_map/ppermute | solution.py:491
  21.2 6.4 %collective-permute-start.6 = (f32[2,128,384]{2,1,0:T(8,128)S(1)}, f32[2,128,384]{2,1,0:T(8,128)S(1)}, u32[]{:S(2)}, u32[]{:S(2)}) collective-permute-start(f32[2,128,384]{2,1,0:T(8,128)S(1)} %get-tuple-element.45.own_ref), channel_id=1, source_target_pairs={{0,1},{1,0},{2,3},{3,2},{4,5},{5,4},{6,7},{7,6},{8,9},{9,8},{10,11... | collective-permute-start | bytes 1179656 | tf_op jit(solution)/shard_map/ppermute | solution.py:491
  25.8 4.7 %collective-permute-start.5 = (f32[2,128,128]{2,1,0:T(8,128)S(1)}, f32[2,128,128]{2,1,0:T(8,128)S(1)}, u32[]{:S(2)}, u32[]{:S(2)}) collective-permute-start(f32[2,128,128]{2,1,0:T(8,128)S(1)} %get-tuple-element.43.own_ref), channel_id=1, source_target_pairs={{0,1},{1,0},{2,3},{3,2},{4,5},{5,4},{6,7},{7,6},{8,9},{9,8},{10,11... | collective-permute-start | bytes 393224 | tf_op jit(solution)/shard_map/ppermute | solution.py:491
  30.9 7.2 %collective-permute-start.8 = (f32[2,64,640]{2,1,0:T(8,128)S(1)}, f32[2,64,640]{2,1,0:T(8,128)S(1)}, u32[]{:S(2)}, u32[]{:S(2)}) collective-permute-start(f32[2,64,640]{2,1,0:T(8,128)S(1)} %get-tuple-element.51.own_ref), channel_id=1, source_target_pairs={{0,1},{1,0},{2,3},{3,2},{4,5},{5,4},{6,7},{7,6},{8,9},{9,8},{10,11... | collective-permute-start | bytes 983048 | tf_op jit(solution)/shard_map/ppermute | solution.py:491
  31.0 4.7 %collective-permute-start.9 = (bf16[2,64,128]{2,1,0:T(8,128)(2,1)S(1)}, bf16[2,64,128]{2,1,0:T(8,128)(2,1)S(1)}, u32[]{:S(2)}, u32[]{:S(2)}) collective-permute-start(bf16[2,64,128]{2,1,0:T(8,128)(2,1)S(1)} %get-tuple-element.52), channel_id=1, source_target_pairs={{0,96},{32,64},{64,32},{96,0},{128,224},{160,192},{192,160},{224,1... | collective-permute-start | bytes 98312 | tf_op jit(solution)/shard_map/ppermute | solution.py:503
  32.7 8.0 %collective-permute-start.7 = (bf16[2,64,512]{2,1,0:T(8,128)(2,1)S(1)}, bf16[2,64,512]{2,1,0:T(8,128)(2,1)S(1)}, u32[]{:S(2)}, u32[]{:S(2)}) collective-permute-start(bf16[2,64,512]{2,1,0:T(8,128)(2,1)S(1)} %get-tuple-element.50), channel_id=1, source_target_pairs={{0,96},{32,64},{64,32},{96,0},{128,224},{160,192},{192,160},{224,1... | collective-permute-start | bytes 393224 | tf_op jit(solution)/shard_map/ppermute | solution.py:503
  35.8 2.4 %collective-permute-start.10 = (bf16[2,64,128]{2,1,0:T(8,128)(2,1)S(1)}, bf16[2,64,128]{2,1,0:T(8,128)(2,1)S(1)}, u32[]{:S(2)}, u32[]{:S(2)}) collective-permute-start(bf16[2,64,128]{2,1,0:T(8,128)(2,1)S(1)} %collective-permute-done.9.far_ref), channel_id=1, source_target_pairs={{0,1},{1,0},{2,3},{3,2},{4,5},{5,4},{6,7},{7,6},{8,9},{9,8},{10,11... | collective-permute-start | bytes 98312 | tf_op jit(solution)/shard_map/ppermute | solution.py:491
  40.7 1.4 %collective-permute-start.11 = (bf16[2,64,512]{2,1,0:T(8,128)(2,1)S(1)}, bf16[2,64,512]{2,1,0:T(8,128)(2,1)S(1)}, u32[]{:S(2)}, u32[]{:S(2)}) collective-permute-start(bf16[2,64,512]{2,1,0:T(8,128)(2,1)S(1)} %collective-permute-done.7.far_ref), channel_id=1, source_target_pairs={{0,1},{1,0},{2,3},{3,2},{4,5},{5,4},{6,7},{7,6},{8,9},{9,8},{10,11... | collective-permute-start | bytes 393224 | tf_op jit(solution)/shard_map/ppermute | solution.py:491

commit v2 on v1

--- a/solution.py
+++ b/solution.py
@@ -78,7 +78,7 @@
     for k in range(1, SQUARINGS):
         last = k + 1 == SQUARINGS
         both = total if last else jnp.concatenate([power, total], axis=1)
-        if k < 3:
+        if k < 2:
             step = dot_split(split(power), split(both))
         else:
             step = dot(power.astype(B16), both.astype(B16))
@@ -99,7 +99,7 @@
         both = total
         if k + 1 < SQUARINGS:
             both = jnp.concatenate([power, total], axis=1)
-        if k < 3:
+        if k < 2:
             step = complex_dot(power, both)
         else:
             step = dot(embed(power.astype(B16)), both.astype(B16))
@@ -194,52 +194,17 @@
 COSTS = (5.0, 3.0, 0.4, 0.8, 3.0)
 BLOCK = 16
 BLOCKS = SEG // BLOCK
-AHEAD = 3
-
-
-def stencil_kernel(
-    source_ref, guess_ref, coef_ref, body_ref, flat_ref, body_out, source, guess, coef_rows,
-    source_sems, guess_sems, body_sems, coef_sem,
-):
+
+
+def stencil_kernel(source, guess, coef_rows, flat_ref, diagonal_ref):
     width = 2 * SEG
     chunk = BLOCK * width
     span = BLOCK * SEG
-
-    def source_copy(i):
-        rows = pl.ds(i * chunk, chunk)
-        return pltpu.make_async_copy(source_ref.at[rows], source.at[rows], source_sems.at[i])
-
-    def guess_copy(i):
-        rows = pl.ds(i * chunk, chunk)
-        return pltpu.make_async_copy(guess_ref.at[rows], guess.at[rows], guess_sems.at[i])
-
-    def body_copy(i):
-        rows = pl.ds(i * (512 // BLOCKS), 512 // BLOCKS)
-        return pltpu.make_async_copy(body_ref.at[rows], body_out.at[rows], body_sems.at[i])
-
-    coef_copy = pltpu.make_async_copy(coef_ref, coef_rows, coef_sem)
-    coef_copy.start()
-    for i in range(AHEAD):
-        guess_copy(i).start()
-        source_copy(i).start()
     table = stencil_matrix()
     planes = planes_matrix()
-    coef_copy.wait()
-    guess_copy(0).wait()
+    diagonal_ref[...] = coef_rows[...]
 
     def block(i, carry):
-        @pl.when(i + AHEAD < BLOCKS)
-        def _():
-            guess_copy(i + AHEAD).start()
-            source_copy(i + AHEAD).start()
-
-        body_copy(i).start()
-
-        @pl.when(i + 1 < BLOCKS)
-        def _():
-            guess_copy(i + 1).wait()
-
-        source_copy(i).wait()
         base = i * chunk
 
         def rows_at(ref, begin):
@@ -280,8 +245,6 @@
         return carry
 
     lax.fori_loop(0, BLOCKS, block, 0)
-    for i in range(BLOCKS):
-        body_copy(i).wait()
 
 
 def leaf_kernel(
@@ -450,8 +413,10 @@
     near = sides_of(own_ref, mate_ref)
     far = sides_of(far_ref, far_mate_ref)
     rows = stack(out_ref, 0, SEG)
-    inverse = neumann(complex_dot(far, near[:, :128]))
-    bounced = complex_dot(far, near[:, 128:])
+    exact = embed(far.astype(WIRE))
+    reflected = dot(exact, split(near)[0]) + dot(exact, split(near)[1])
+    inverse = neumann(reflected[:, :128])
+    bounced = reflected[:, 128:]
     carried = complex_dot(rows[:, :128], inverse)
     store_stacked(carried_ref, carried)
     store_stacked(mine_ref, rows[:, 128:] + complex_dot(carried, bounced))
@@ -517,16 +482,11 @@
     across_k = swap_far(row_k, "tx")
     across_l = swap_far(col_l, "ty")
     across_j = swap_near(col_j, "ty")
-    flat, body = call(
-        stencil_kernel, "stencil",
-        [((SEG * SEG, 2 * RHS), F32), ((512, SEG * SEG), B16)],
-        source.reshape(SEG * SEG * 2, RHS), guess.reshape(SEG * SEG * 2, RHS), coefficient,
-        body_map.reshape(512, SEG * SEG), kept=4, cost=1.0,
-        scratch=[
-            pltpu.VMEM((SEG * SEG * 2, RHS), B16), pltpu.VMEM((SEG * SEG * 2, RHS), B16),
-            pltpu.VMEM((SEG, SEG), F32), dma((BLOCKS,)), dma((BLOCKS,)), dma((BLOCKS,)), dma(()),
-        ],
-    )
+    flat, _ = call(
+        stencil_kernel, "stencil", [((SEG * SEG, 2 * RHS), F32), ((SEG, SEG), F32)],
+        source.reshape(SEG * SEG * 2, RHS), guess.reshape(SEG * SEG * 2, RHS), coefficient, cost=1.0,
+    )
+    body = body_map.reshape(512, SEG * SEG)
     own_load, sent_load = call(
         leaf_kernel, "leaf_loads", [((2, 256, RHS), F32), ((2, 192, RHS), WIRE)],
         flat, body, across_j, across_k, across_l, partner, cost=2.5,

time: 43.3 us -> 41.3 us (0.954)
  Pallas kernels: 18.1 us -> 16 us
    pallas_call x9, Pallas kernels: 18.1 us -> 16 us  [call(): pl.pallas_call(kernel, in_specs=[pl.BlockSpec(memory_space=pltpu.HBM if i...]
  transfers between devices with their start and end apart: 12 -> 12, of which waited for: 3 -> 3; matrix products, arithmetic and copies ran while one was open for 0% -> 0% of each run, Pallas kernels for 31% -> 27%
where the time goes in v2:
time: 41.3 us; the launch traced here: 41.2 us
  starting transfers between devices  21.2 us (51%)
  Pallas kernels  16 us (39%)
  waiting for transfers between devices  3.29 us (8%)
  between operations  0.77 us (2%)
    pallas_call x9, Pallas kernels, call(): pl.pallas_call(kernel, in_specs=[pl.BlockSpec(memory_space=pltpu.HBM if i...  16 us
    ppermute x8, starting transfers between devices, swap_near(): lax.ppermute(value, axis, [(i, i ^ 1) for i in range(lax.axis_size(axis))])  12 us
    ppermute x2, starting transfers between devices, swap_far(): return lax.ppermute(value, axis, pairs)  5.85 us
    ppermute x2, starting transfers between devices, from_other_half(): lax.ppermute(value, 'tx', [(i, i ^ 3) for i in range(lax.axis_size('tx'))])  3.34 us
    ppermute x8, waiting for transfers between devices, swap_near(): lax.ppermute(value, axis, [(i, i ^ 1) for i in range(lax.axis_size(axis))])  1.88 us
    ppermute x2, waiting for transfers between devices, from_other_half(): lax.ppermute(value, 'tx', [(i, i ^ 3) for i in range(lax.axis_size('tx'))])  1.41 us
  transfers between devices with their start and end apart: 12, of which 3 were waited for; matrix products, arithmetic and copies ran while one was open for 0% of the time, Pallas kernels for 27%

profile of v2, /device:TPU:1, one launch (start us, length us, event | category | flops | bytes accessed | tf_op | source)
XLA Modules:
  0.0 41.2 jit_solution(7983261974440992344)
XLA Ops:
  0.6 0.0 copy-start
  0.6 0.0 copy-start.2
  0.7 0.0 copy-start.1
  0.7 0.0 copy-start.3
  0.7 1.5 %front.1 = (bf16[64,2,128]{2,1,0:T(2,128)(2,1)S(1)}, bf16[64,2,128]{2,1,0:T(2,128)(2,1)S(1)}, bf16[64,2,128]{2,1,0:T(2,128)(2,1)S(1)}, f32[2,256,256]{2,1,0:T(8,128)S(1)}, bf16[896,128]{1,0:T(8,128)(2,1)S(1)}) custom-call(bf16[64,64,2,128]{3,2,1,0:T(2,128)(2,1)} %guess_ref.1, bf16[8192,128]{1,0:T(8,128)(2,1)} %bitcast.9, f32[2,256,256]{2,1,0:T(8,128)} %bitcast.16), custom_call_target="tpu_custom_call" | custom-call | flops 1100000000 | tf_op jit(solution)/shard_map/front/pallas_call | solution.py:444
  2.2 2.6 %collective-permute-start.3 = (bf16[896,128]{1,0:T(8,128)(2,1)S(1)}, bf16[896,128]{1,0:T(8,128)(2,1)S(1)}, u32[]{:S(2)}, u32[]{:S(2)}) collective-permute-start(bf16[896,128]{1,0:T(8,128)(2,1)S(1)} %get-tuple-element.34), channel_id=1, source_target_pairs={{0,32},{32,0},{64,96},{96,64},{128,160},{160,128},{192,224},{224,1... | collective-permute-start | bytes 688136 | tf_op jit(solution)/shard_map/ppermute | solution.py:456
  4.7 4.7 %collective-permute-start.1 = (bf16[128,128]{1,0:T(8,128)(2,1)S(1)}, bf16[128,128]{1,0:T(8,128)(2,1)S(1)}, u32[]{:S(2)}, u32[]{:S(2)}) collective-permute-start(bf16[128,128]{1,0:T(8,128)(2,1)S(1)} %bitcast.15), channel_id=1, source_target_pairs={{32,64},{64,32},{96,128},{128,96},{160,192},{192,160},{224,0},{0,2... | collective-permute-start | bytes 98312 | tf_op jit(solution)/shard_map/ppermute | solution.py:464
  9.4 1.2 %collective-permute-start = (bf16[128,128]{1,0:T(8,128)(2,1)S(1)}, bf16[128,128]{1,0:T(8,128)(2,1)S(1)}, u32[]{:S(2)}, u32[]{:S(2)}) collective-permute-start(bf16[128,128]{1,0:T(8,128)(2,1)S(1)} %bitcast.14), channel_id=1, source_target_pairs={{0,1},{1,0},{2,3},{3,2},{4,5},{5,4},{6,7},{7,6},{8,9},{9,8},{10,11... | collective-permute-start | bytes 98312 | tf_op jit(solution)/shard_map/ppermute | solution.py:456
  10.6 1.2 %collective-permute-start.2 = (bf16[128,128]{1,0:T(8,128)(2,1)S(1)}, bf16[128,128]{1,0:T(8,128)(2,1)S(1)}, u32[]{:S(2)}, u32[]{:S(2)}) collective-permute-start(bf16[128,128]{1,0:T(8,128)(2,1)S(1)} %bitcast.13), channel_id=1, source_target_pairs={{1,2},{2,1},{3,4},{4,3},{5,6},{6,5},{7,8},{8,7},{9,10},{10,9},{11,... | collective-permute-start | bytes 98312 | tf_op jit(solution)/shard_map/ppermute | solution.py:464
  11.8 0.0 copy-done
  11.8 0.0 copy-done.2
  11.8 0.0 copy-done.1
  11.8 2.7 %stencil.1 = (f32[4096,256]{1,0:T(8,128)S(1)}, f32[64,64]{1,0:T(8,128)}) custom-call(bf16[8192,128]{1,0:T(8,128)(2,1)S(1)} %bitcast.11, bf16[8192,128]{1,0:T(8,128)(2,1)S(1)} %bitcast.10, f32[64,64]{1,0:T(8,128)S(1)} %copy-done.2), custom_call_target="tpu_custom_call" | custom-call | flops 1100000000 | tf_op jit(solution)/shard_map/stencil/pallas_call | solution.py:444
  14.5 0.0 collective-permute-done.1.across_k
  14.5 0.0 collective-permute-done.across_j
  14.5 0.0 collective-permute-done.2.across_l
  14.5 0.0 collective-permute-done.3.partner_ref
  14.5 0.0 copy-done.3
  14.5 2.0 %leaf_loads.1 = (f32[2,256,128]{2,1,0:T(8,128)S(1)}, bf16[2,192,128]{2,1,0:T(8,128)(2,1)S(1)}) custom-call(f32[4096,256]{1,0:T(8,128)S(1)} %get-tuple-element.30.flat_ref, bf16[512,4096]{1,0:T(8,128)(2,1)S(1)} %bitcast.12, bf16[128,128]{1,0:T(8,128)(2,1)S(1)} %collective-permute-done.across_j, bf16[128,128]{1,0:T(8,128)(2,1)S(1)} %collective-permute-done.1.across_k, ...), custom_call_target="tpu_custom_call" | custom-call | flops 2750000128 | tf_op jit(solution)/shard_map/leaf_loads/pallas_call | solution.py:444
  16.5 0.1 collective-permute-start.4
  16.6 2.8 %merge_rows.1 = (f32[2,128,384]{2,1,0:T(8,128)S(1)}, f32[2,128,384]{2,1,0:T(8,128)S(1)}, f32[2,256,128]{2,1,0:T(8,128)S(1)}) custom-call(f32[2,256,256]{2,1,0:T(8,128)S(1)} %get-tuple-element.38.own_ref, bf16[896,128]{1,0:T(8,128)(2,1)S(1)} %collective-permute-done.3.partner_ref), custom_call_target="tpu_custom_call" | custom-call | flops 3300000000 | tf_op jit(solution)/shard_map/merge_rows/pallas_call | solution.py:444
  19.3 4.2 %collective-permute-start.6 = (f32[2,128,384]{2,1,0:T(8,128)S(1)}, f32[2,128,384]{2,1,0:T(8,128)S(1)}, u32[]{:S(2)}, u32[]{:S(2)}) collective-permute-start(f32[2,128,384]{2,1,0:T(8,128)S(1)} %get-tuple-element.43.own_ref), channel_id=1, source_target_pairs={{0,1},{1,0},{2,3},{3,2},{4,5},{5,4},{6,7},{7,6},{8,9},{9,8},{10,11... | collective-permute-start | bytes 1179656 | tf_op jit(solution)/shard_map/ppermute | solution.py:456
  23.6 0.0 collective-permute-done.4.partner_ref
  23.6 0.4 load_rows.1
  24.0 1.8 %collective-permute-start.5 = (f32[2,128,128]{2,1,0:T(8,128)S(1)}, f32[2,128,128]{2,1,0:T(8,128)S(1)}, u32[]{:S(2)}, u32[]{:S(2)}) collective-permute-start(f32[2,128,128]{2,1,0:T(8,128)S(1)} %get-tuple-element.41.own_ref), channel_id=1, source_target_pairs={{0,1},{1,0},{2,3},{3,2},{4,5},{5,4},{6,7},{7,6},{8,9},{9,8},{10,11... | collective-permute-start | bytes 393224 | tf_op jit(solution)/shard_map/ppermute | solution.py:456
  25.8 0.0 collective-permute-done.6.across_ref
  25.8 2.8 %merge_cols.1 = (f32[2,64,512]{2,1,0:T(8,128)S(1)}, bf16[2,64,128]{2,1,0:T(8,128)(2,1)S(1)}, f32[2,64,512]{2,1,0:T(8,128)S(1)}, f32[2,128,256]{2,1,0:T(8,128)S(1)}) custom-call(f32[2,128,384]{2,1,0:T(8,128)S(1)} %get-tuple-element.43.own_ref, f32[2,128,384]{2,1,0:T(8,128)S(1)} %collective-permute-done.6.across_ref, f32[2,128,384]{2,1,0:T(8,128)S(1)} %get-tuple-element.44.keep_ref), custom_call_target="tpu_custom_call" | custom-call | flops 3300000000 | tf_op jit(solution)/shard_map/merge_cols/pallas_call | solution.py:444
  28.6 0.0 collective-permute-done.5.across_ref
  28.6 0.4 load_cols.1
  29.0 0.1 collective-permute-start.8
  29.1 1.7 %collective-permute-start.9 = (bf16[2,64,128]{2,1,0:T(8,128)(2,1)S(1)}, bf16[2,64,128]{2,1,0:T(8,128)(2,1)S(1)}, u32[]{:S(2)}, u32[]{:S(2)}) collective-permute-start(bf16[2,64,128]{2,1,0:T(8,128)(2,1)S(1)} %get-tuple-element.50), channel_id=1, source_target_pairs={{0,96},{32,64},{64,32},{96,0},{128,224},{160,192},{192,160},{224,1... | collective-permute-start | bytes 98312 | tf_op jit(solution)/shard_map/ppermute | solution.py:468
  30.8 1.6 %collective-permute-start.7 = (bf16[2,64,512]{2,1,0:T(8,128)(2,1)S(1)}, bf16[2,64,512]{2,1,0:T(8,128)(2,1)S(1)}, u32[]{:S(2)}, u32[]{:S(2)}) collective-permute-start(bf16[2,64,512]{2,1,0:T(8,128)(2,1)S(1)} %get-tuple-element.48), channel_id=1, source_target_pairs={{0,96},{32,64},{64,32},{96,0},{128,224},{160,192},{192,160},{224,1... | collective-permute-start | bytes 393224 | tf_op jit(solution)/shard_map/ppermute | solution.py:468
  32.5 1.4 %collective-permute-done.9.far_ref = bf16[2,64,128]{2,1,0:T(8,128)(2,1)S(1)} collective-permute-done((bf16[2,64,128]{2,1,0:T(8,128)(2,1)S(1)}, bf16[2,64,128]{2,1,0:T(8,128)(2,1)S(1)}, u32[]{:S(2)}, u32[]{:S(2)}) %collective-permute-start.9) | collective-permute-done | bytes 32800 | tf_op jit(solution)/shard_map/ppermute | solution.py:468
  33.9 1.5 %collective-permute-start.10 = (bf16[2,64,128]{2,1,0:T(8,128)(2,1)S(1)}, bf16[2,64,128]{2,1,0:T(8,128)(2,1)S(1)}, u32[]{:S(2)}, u32[]{:S(2)}) collective-permute-start(bf16[2,64,128]{2,1,0:T(8,128)(2,1)S(1)} %collective-permute-done.9.far_ref), channel_id=1, source_target_pairs={{0,1},{1,0},{2,3},{3,2},{4,5},{5,4},{6,7},{7,6},{8,9},{9,8},{10,11... | collective-permute-start | bytes 98312 | tf_op jit(solution)/shard_map/ppermute | solution.py:456
  35.4 0.9 %collective-permute-done.10.far_mate_ref = bf16[2,64,128]{2,1,0:T(8,128)(2,1)S(1)} collective-permute-done((bf16[2,64,128]{2,1,0:T(8,128)(2,1)S(1)}, bf16[2,64,128]{2,1,0:T(8,128)(2,1)S(1)}, u32[]{:S(2)}, u32[]{:S(2)}) %collective-permute-start.10) | collective-permute-done | bytes 32800 | tf_op jit(solution)/shard_map/ppermute | solution.py:456
  36.2 0.0 collective-permute-done.8.mate_ref
  36.2 2.5 %top_solve.1 = (f32[2,64,128]{2,1,0:T(8,128)S(1)}, f32[2,64,512]{2,1,0:T(8,128)S(1)}) custom-call(f32[2,64,640]{2,1,0:T(8,128)S(1)} %get-tuple-element.49.own_ref, f32[2,64,640]{2,1,0:T(8,128)S(1)} %collective-permute-done.8.mate_ref, bf16[2,64,128]{2,1,0:T(8,128)(2,1)S(1)} %collective-permute-done.9.far_ref, ...), custom_call_target="tpu_custom_call" | custom-call | flops 880000000 | tf_op jit(solution)/shard_map/top_solve/pallas_call | solution.py:444
  38.8 0.0 collective-permute-done.7.far_ref
  38.8 0.4 %collective-permute-start.11 = (bf16[2,64,512]{2,1,0:T(8,128)(2,1)S(1)}, bf16[2,64,512]{2,1,0:T(8,128)(2,1)S(1)}, u32[]{:S(2)}, u32[]{:S(2)}) collective-permute-start(bf16[2,64,512]{2,1,0:T(8,128)(2,1)S(1)} %collective-permute-done.7.far_ref), channel_id=1, source_target_pairs={{0,1},{1,0},{2,3},{3,2},{4,5},{5,4},{6,7},{7,6},{8,9},{9,8},{10,11... | collective-permute-start | bytes 393224 | tf_op jit(solution)/shard_map/ppermute | solution.py:456
  39.2 1.0 %collective-permute-done.11.far_mate_ref = bf16[2,64,512]{2,1,0:T(8,128)(2,1)S(1)} collective-permute-done((bf16[2,64,512]{2,1,0:T(8,128)(2,1)S(1)}, bf16[2,64,512]{2,1,0:T(8,128)(2,1)S(1)}, u32[]{:S(2)}, u32[]{:S(2)}) %collective-permute-start.11) | collective-permute-done | bytes 131104 | tf_op jit(solution)/shard_map/ppermute | solution.py:456
  40.2 1.0 %merge_top.1 = (f32[2,64,768]{2,1,0:T(8,128)}, f32[2,64,128]{2,1,0:T(8,128)}) custom-call(f32[2,64,128]{2,1,0:T(8,128)S(1)} %get-tuple-element.53.carried_ref, f32[2,64,512]{2,1,0:T(8,128)S(1)} %get-tuple-element.54.mine_ref, bf16[2,64,512]{2,1,0:T(8,128)(2,1)S(1)} %collective-permute-done.7.far_ref, bf16[2,64,512]{2,1,0:T(8,128)(2,1)S(1)} %collective-permute-done.11.far_mate_ref), custom_call_target="tpu_custom_call" | custom-call | flops 1100000000 | tf_op jit(solution)/shard_map/merge_top/pallas_call | solution.py:444
Async XLA Ops:
  0.6 11.2 %copy-start = (bf16[64,64,2,128]{3,2,1,0:T(2,128)(2,1)S(1)}, bf16[64,64,2,128]{3,2,1,0:T(2,128)(2,1)}, u32[]{:S(2)}) copy-start(bf16[64,64,2,128]{3,2,1,0:T(2,128)(2,1)} %guess_ref.1) | copy-start | bytes 6291460
  0.6 11.2 %copy-start.2 = (f32[64,64]{1,0:T(8,128)S(1)}, f32[64,64]{1,0:T(8,128)}, u32[]{:S(2)}) copy-start(f32[64,64]{1,0:T(8,128)} %coef_rows.1) | copy-start | bytes 49156
  0.7 11.2 %copy-start.1 = (bf16[64,64,2,128]{3,2,1,0:T(2,128)(2,1)S(1)}, bf16[64,64,2,128]{3,2,1,0:T(2,128)(2,1)}, u32[]{:S(2)}) copy-start(bf16[64,64,2,128]{3,2,1,0:T(2,128)(2,1)} %param.5) | copy-start | bytes 6291460
  0.7 13.8 %copy-start.3 = (bf16[1,1,2,256,4096]{4,3,2,1,0:T(8,128)(2,1)S(1)}, bf16[1,1,2,256,4096]{4,3,2,1,0:T(8,128)(2,1)}, u32[]{:S(2)}) copy-start(bf16[1,1,2,256,4096]{4,3,2,1,0:T(8,128)(2,1)} %param.9) | copy-start | bytes 12582916
  2.2 12.3 %collective-permute-start.3 = (bf16[896,128]{1,0:T(8,128)(2,1)S(1)}, bf16[896,128]{1,0:T(8,128)(2,1)S(1)}, u32[]{:S(2)}, u32[]{:S(2)}) collective-permute-start(bf16[896,128]{1,0:T(8,128)(2,1)S(1)} %get-tuple-element.34), channel_id=1, source_target_pairs={{0,32},{32,0},{64,96},{96,64},{128,160},{160,128},{192,224},{224,1... | collective-permute-start | bytes 688136 | tf_op jit(solution)/shard_map/ppermute | solution.py:456
  4.7 9.8 %collective-permute-start.1 = (bf16[128,128]{1,0:T(8,128)(2,1)S(1)}, bf16[128,128]{1,0:T(8,128)(2,1)S(1)}, u32[]{:S(2)}, u32[]{:S(2)}) collective-permute-start(bf16[128,128]{1,0:T(8,128)(2,1)S(1)} %bitcast.15), channel_id=1, source_target_pairs={{32,64},{64,32},{96,128},{128,96},{160,192},{192,160},{224,0},{0,2... | collective-permute-start | bytes 98312 | tf_op jit(solution)/shard_map/ppermute | solution.py:464
  9.4 5.1 %collective-permute-start = (bf16[128,128]{1,0:T(8,128)(2,1)S(1)}, bf16[128,128]{1,0:T(8,128)(2,1)S(1)}, u32[]{:S(2)}, u32[]{:S(2)}) collective-permute-start(bf16[128,128]{1,0:T(8,128)(2,1)S(1)} %bitcast.14), channel_id=1, source_target_pairs={{0,1},{1,0},{2,3},{3,2},{4,5},{5,4},{6,7},{7,6},{8,9},{9,8},{10,11... | collective-permute-start | bytes 98312 | tf_op jit(solution)/shard_map/ppermute | solution.py:456
  10.6 3.9 %collective-permute-start.2 = (bf16[128,128]{1,0:T(8,128)(2,1)S(1)}, bf16[128,128]{1,0:T(8,128)(2,1)S(1)}, u32[]{:S(2)}, u32[]{:S(2)}) collective-permute-start(bf16[128,128]{1,0:T(8,128)(2,1)S(1)} %bitcast.13), channel_id=1, source_target_pairs={{1,2},{2,1},{3,4},{4,3},{5,6},{6,5},{7,8},{8,7},{9,10},{10,9},{11,... | collective-permute-start | bytes 98312 | tf_op jit(solution)/shard_map/ppermute | solution.py:464
  16.5 7.1 %collective-permute-start.4 = (bf16[2,192,128]{2,1,0:T(8,128)(2,1)S(1)}, bf16[2,192,128]{2,1,0:T(8,128)(2,1)S(1)}, u32[]{:S(2)}, u32[]{:S(2)}) collective-permute-start(bf16[2,192,128]{2,1,0:T(8,128)(2,1)S(1)} %get-tuple-element.37), channel_id=1, source_target_pairs={{0,32},{32,0},{64,96},{96,64},{128,160},{160,128},{192,224},{224,1... | collective-permute-start | bytes 294920 | tf_op jit(solution)/shard_map/ppermute | solution.py:456
  19.3 6.4 %collective-permute-start.6 = (f32[2,128,384]{2,1,0:T(8,128)S(1)}, f32[2,128,384]{2,1,0:T(8,128)S(1)}, u32[]{:S(2)}, u32[]{:S(2)}) collective-permute-start(f32[2,128,384]{2,1,0:T(8,128)S(1)} %get-tuple-element.43.own_ref), channel_id=1, source_target_pairs={{0,1},{1,0},{2,3},{3,2},{4,5},{5,4},{6,7},{7,6},{8,9},{9,8},{10,11... | collective-permute-start | bytes 1179656 | tf_op jit(solution)/shard_map/ppermute | solution.py:456
  24.0 4.7 %collective-permute-start.5 = (f32[2,128,128]{2,1,0:T(8,128)S(1)}, f32[2,128,128]{2,1,0:T(8,128)S(1)}, u32[]{:S(2)}, u32[]{:S(2)}) collective-permute-start(f32[2,128,128]{2,1,0:T(8,128)S(1)} %get-tuple-element.41.own_ref), channel_id=1, source_target_pairs={{0,1},{1,0},{2,3},{3,2},{4,5},{5,4},{6,7},{7,6},{8,9},{9,8},{10,11... | collective-permute-start | bytes 393224 | tf_op jit(solution)/shard_map/ppermute | solution.py:456
  29.0 7.2 %collective-permute-start.8 = (f32[2,64,640]{2,1,0:T(8,128)S(1)}, f32[2,64,640]{2,1,0:T(8,128)S(1)}, u32[]{:S(2)}, u32[]{:S(2)}) collective-permute-start(f32[2,64,640]{2,1,0:T(8,128)S(1)} %get-tuple-element.49.own_ref), channel_id=1, source_target_pairs={{0,1},{1,0},{2,3},{3,2},{4,5},{5,4},{6,7},{7,6},{8,9},{9,8},{10,11... | collective-permute-start | bytes 983048 | tf_op jit(solution)/shard_map/ppermute | solution.py:456
  29.1 4.7 %collective-permute-start.9 = (bf16[2,64,128]{2,1,0:T(8,128)(2,1)S(1)}, bf16[2,64,128]{2,1,0:T(8,128)(2,1)S(1)}, u32[]{:S(2)}, u32[]{:S(2)}) collective-permute-start(bf16[2,64,128]{2,1,0:T(8,128)(2,1)S(1)} %get-tuple-element.50), channel_id=1, source_target_pairs={{0,96},{32,64},{64,32},{96,0},{128,224},{160,192},{192,160},{224,1... | collective-permute-start | bytes 98312 | tf_op jit(solution)/shard_map/ppermute | solution.py:468
  30.8 7.9 %collective-permute-start.7 = (bf16[2,64,512]{2,1,0:T(8,128)(2,1)S(1)}, bf16[2,64,512]{2,1,0:T(8,128)(2,1)S(1)}, u32[]{:S(2)}, u32[]{:S(2)}) collective-permute-start(bf16[2,64,512]{2,1,0:T(8,128)(2,1)S(1)} %get-tuple-element.48), channel_id=1, source_target_pairs={{0,96},{32,64},{64,32},{96,0},{128,224},{160,192},{192,160},{224,1... | collective-permute-start | bytes 393224 | tf_op jit(solution)/shard_map/ppermute | solution.py:468
  33.9 2.4 %collective-permute-start.10 = (bf16[2,64,128]{2,1,0:T(8,128)(2,1)S(1)}, bf16[2,64,128]{2,1,0:T(8,128)(2,1)S(1)}, u32[]{:S(2)}, u32[]{:S(2)}) collective-permute-start(bf16[2,64,128]{2,1,0:T(8,128)(2,1)S(1)} %collective-permute-done.9.far_ref), channel_id=1, source_target_pairs={{0,1},{1,0},{2,3},{3,2},{4,5},{5,4},{6,7},{7,6},{8,9},{9,8},{10,11... | collective-permute-start | bytes 98312 | tf_op jit(solution)/shard_map/ppermute | solution.py:456
  38.8 1.4 %collective-permute-start.11 = (bf16[2,64,512]{2,1,0:T(8,128)(2,1)S(1)}, bf16[2,64,512]{2,1,0:T(8,128)(2,1)S(1)}, u32[]{:S(2)}, u32[]{:S(2)}) collective-permute-start(bf16[2,64,512]{2,1,0:T(8,128)(2,1)S(1)} %collective-permute-done.7.far_ref), channel_id=1, source_target_pairs={{0,1},{1,0},{2,3},{3,2},{4,5},{5,4},{6,7},{7,6},{8,9},{9,8},{10,11... | collective-permute-start | bytes 393224 | tf_op jit(solution)/shard_map/ppermute | solution.py:456

commit v3 on v2

--- a/solution.py
+++ b/solution.py
@@ -78,7 +78,7 @@
     for k in range(1, SQUARINGS):
         last = k + 1 == SQUARINGS
         both = total if last else jnp.concatenate([power, total], axis=1)
-        if k < 2:
+        if k < 1:
             step = dot_split(split(power), split(both))
         else:
             step = dot(power.astype(B16), both.astype(B16))
@@ -99,7 +99,7 @@
         both = total
         if k + 1 < SQUARINGS:
             both = jnp.concatenate([power, total], axis=1)
-        if k < 2:
+        if k < 1:
             step = complex_dot(power, both)
         else:
             step = dot(embed(power.astype(B16)), both.astype(B16))

time: 41.3 us -> 41 us (level)
  transfers between devices with their start and end apart: 12 -> 12, of which waited for: 3 -> 3; matrix products, arithmetic and copies ran while one was open for 0% -> 0% of each run, Pallas kernels for 27% -> 26%
where the time goes in v3:
time: 41 us
  starting transfers between devices  21.2 us (52%)
  Pallas kernels  15.7 us (38%)
  waiting for transfers between devices  3.29 us (8%)
  between operations  0.77 us (2%)
    pallas_call x9, Pallas kernels, call(): pl.pallas_call(kernel, in_specs=[pl.BlockSpec(memory_space=pltpu.HBM if i...  15.7 us
    ppermute x8, starting transfers between devices, swap_near(): lax.ppermute(value, axis, [(i, i ^ 1) for i in range(lax.axis_size(axis))])  12 us
    ppermute x2, starting transfers between devices, swap_far(): return lax.ppermute(value, axis, pairs)  5.85 us
    ppermute x2, starting transfers between devices, from_other_half(): lax.ppermute(value, 'tx', [(i, i ^ 3) for i in range(lax.axis_size('tx'))])  3.34 us
    ppermute x8, waiting for transfers between devices, swap_near(): lax.ppermute(value, axis, [(i, i ^ 1) for i in range(lax.axis_size(axis))])  1.88 us
    ppermute x2, waiting for transfers between devices, from_other_half(): lax.ppermute(value, 'tx', [(i, i ^ 3) for i in range(lax.axis_size('tx'))])  1.41 us
  transfers between devices with their start and end apart: 12, of which 3 were waited for; matrix products, arithmetic and copies ran while one was open for 0% of the time, Pallas kernels for 26%

profile of v3, /device:TPU:1, one launch (start us, length us, event | category | flops | bytes accessed | tf_op | source)
XLA Modules:
  0.0 41.0 jit_solution(6804033406982786141)
XLA Ops:
  0.6 0.0 copy-start
  0.6 0.0 copy-start.2
  0.7 0.0 copy-start.1
  0.7 0.0 copy-start.3
  0.7 1.5 %front.1 = (bf16[64,2,128]{2,1,0:T(2,128)(2,1)S(1)}, bf16[64,2,128]{2,1,0:T(2,128)(2,1)S(1)}, bf16[64,2,128]{2,1,0:T(2,128)(2,1)S(1)}, f32[2,256,256]{2,1,0:T(8,128)S(1)}, bf16[896,128]{1,0:T(8,128)(2,1)S(1)}) custom-call(bf16[64,64,2,128]{3,2,1,0:T(2,128)(2,1)} %guess_ref.1, bf16[8192,128]{1,0:T(8,128)(2,1)} %bitcast.9, f32[2,256,256]{2,1,0:T(8,128)} %bitcast.16), custom_call_target="tpu_custom_call" | custom-call | flops 1100000000 | tf_op jit(solution)/shard_map/front/pallas_call | solution.py:444
  2.2 2.6 %collective-permute-start.3 = (bf16[896,128]{1,0:T(8,128)(2,1)S(1)}, bf16[896,128]{1,0:T(8,128)(2,1)S(1)}, u32[]{:S(2)}, u32[]{:S(2)}) collective-permute-start(bf16[896,128]{1,0:T(8,128)(2,1)S(1)} %get-tuple-element.34), channel_id=1, source_target_pairs={{0,32},{32,0},{64,96},{96,64},{128,160},{160,128},{192,224},{224,1... | collective-permute-start | bytes 688136 | tf_op jit(solution)/shard_map/ppermute | solution.py:456
  4.7 4.7 %collective-permute-start.1 = (bf16[128,128]{1,0:T(8,128)(2,1)S(1)}, bf16[128,128]{1,0:T(8,128)(2,1)S(1)}, u32[]{:S(2)}, u32[]{:S(2)}) collective-permute-start(bf16[128,128]{1,0:T(8,128)(2,1)S(1)} %bitcast.15), channel_id=1, source_target_pairs={{32,64},{64,32},{96,128},{128,96},{160,192},{192,160},{224,0},{0,2... | collective-permute-start | bytes 98312 | tf_op jit(solution)/shard_map/ppermute | solution.py:464
  9.4 1.2 %collective-permute-start = (bf16[128,128]{1,0:T(8,128)(2,1)S(1)}, bf16[128,128]{1,0:T(8,128)(2,1)S(1)}, u32[]{:S(2)}, u32[]{:S(2)}) collective-permute-start(bf16[128,128]{1,0:T(8,128)(2,1)S(1)} %bitcast.14), channel_id=1, source_target_pairs={{0,1},{1,0},{2,3},{3,2},{4,5},{5,4},{6,7},{7,6},{8,9},{9,8},{10,11... | collective-permute-start | bytes 98312 | tf_op jit(solution)/shard_map/ppermute | solution.py:456
  10.6 1.2 %collective-permute-start.2 = (bf16[128,128]{1,0:T(8,128)(2,1)S(1)}, bf16[128,128]{1,0:T(8,128)(2,1)S(1)}, u32[]{:S(2)}, u32[]{:S(2)}) collective-permute-start(bf16[128,128]{1,0:T(8,128)(2,1)S(1)} %bitcast.13), channel_id=1, source_target_pairs={{1,2},{2,1},{3,4},{4,3},{5,6},{6,5},{7,8},{8,7},{9,10},{10,9},{11,... | collective-permute-start | bytes 98312 | tf_op jit(solution)/shard_map/ppermute | solution.py:464
  11.8 0.0 copy-done
  11.8 0.0 copy-done.2
  11.8 0.0 copy-done.1
  11.8 2.7 %stencil.1 = (f32[4096,256]{1,0:T(8,128)S(1)}, f32[64,64]{1,0:T(8,128)}) custom-call(bf16[8192,128]{1,0:T(8,128)(2,1)S(1)} %bitcast.11, bf16[8192,128]{1,0:T(8,128)(2,1)S(1)} %bitcast.10, f32[64,64]{1,0:T(8,128)S(1)} %copy-done.2), custom_call_target="tpu_custom_call" | custom-call | flops 1100000000 | tf_op jit(solution)/shard_map/stencil/pallas_call | solution.py:444
  14.5 0.0 collective-permute-done.1.across_k
  14.5 0.0 collective-permute-done.across_j
  14.5 0.0 collective-permute-done.2.across_l
  14.5 0.0 collective-permute-done.3.partner_ref
  14.5 0.0 copy-done.3
  14.5 2.0 %leaf_loads.1 = (f32[2,256,128]{2,1,0:T(8,128)S(1)}, bf16[2,192,128]{2,1,0:T(8,128)(2,1)S(1)}) custom-call(f32[4096,256]{1,0:T(8,128)S(1)} %get-tuple-element.30.flat_ref, bf16[512,4096]{1,0:T(8,128)(2,1)S(1)} %bitcast.12, bf16[128,128]{1,0:T(8,128)(2,1)S(1)} %collective-permute-done.across_j, bf16[128,128]{1,0:T(8,128)(2,1)S(1)} %collective-permute-done.1.across_k, ...), custom_call_target="tpu_custom_call" | custom-call | flops 2750000128 | tf_op jit(solution)/shard_map/leaf_loads/pallas_call | solution.py:444
  16.5 0.1 collective-permute-start.4
  16.6 2.7 %merge_rows.1 = (f32[2,128,384]{2,1,0:T(8,128)S(1)}, f32[2,128,384]{2,1,0:T(8,128)S(1)}, f32[2,256,128]{2,1,0:T(8,128)S(1)}) custom-call(f32[2,256,256]{2,1,0:T(8,128)S(1)} %get-tuple-element.38.own_ref, bf16[896,128]{1,0:T(8,128)(2,1)S(1)} %collective-permute-done.3.partner_ref), custom_call_target="tpu_custom_call" | custom-call | flops 3300000000 | tf_op jit(solution)/shard_map/merge_rows/pallas_call | solution.py:444
  19.3 4.2 %collective-permute-start.6 = (f32[2,128,384]{2,1,0:T(8,128)S(1)}, f32[2,128,384]{2,1,0:T(8,128)S(1)}, u32[]{:S(2)}, u32[]{:S(2)}) collective-permute-start(f32[2,128,384]{2,1,0:T(8,128)S(1)} %get-tuple-element.43.own_ref), channel_id=1, source_target_pairs={{0,1},{1,0},{2,3},{3,2},{4,5},{5,4},{6,7},{7,6},{8,9},{9,8},{10,11... | collective-permute-start | bytes 1179656 | tf_op jit(solution)/shard_map/ppermute | solution.py:456
  23.5 0.0 collective-permute-done.4.partner_ref
  23.5 0.4 load_rows.1
  23.9 1.9 %collective-permute-start.5 = (f32[2,128,128]{2,1,0:T(8,128)S(1)}, f32[2,128,128]{2,1,0:T(8,128)S(1)}, u32[]{:S(2)}, u32[]{:S(2)}) collective-permute-start(f32[2,128,128]{2,1,0:T(8,128)S(1)} %get-tuple-element.41.own_ref), channel_id=1, source_target_pairs={{0,1},{1,0},{2,3},{3,2},{4,5},{5,4},{6,7},{7,6},{8,9},{9,8},{10,11... | collective-permute-start | bytes 393224 | tf_op jit(solution)/shard_map/ppermute | solution.py:456
  25.8 0.0 collective-permute-done.6.across_ref
  25.8 2.7 %merge_cols.1 = (f32[2,64,512]{2,1,0:T(8,128)S(1)}, bf16[2,64,128]{2,1,0:T(8,128)(2,1)S(1)}, f32[2,64,512]{2,1,0:T(8,128)S(1)}, f32[2,128,256]{2,1,0:T(8,128)S(1)}) custom-call(f32[2,128,384]{2,1,0:T(8,128)S(1)} %get-tuple-element.43.own_ref, f32[2,128,384]{2,1,0:T(8,128)S(1)} %collective-permute-done.6.across_ref, f32[2,128,384]{2,1,0:T(8,128)S(1)} %get-tuple-element.44.keep_ref), custom_call_target="tpu_custom_call" | custom-call | flops 3300000000 | tf_op jit(solution)/shard_map/merge_cols/pallas_call | solution.py:444
  28.5 0.0 collective-permute-done.5.across_ref
  28.5 0.4 load_cols.1
  28.9 0.1 collective-permute-start.8
  29.0 1.7 %collective-permute-start.9 = (bf16[2,64,128]{2,1,0:T(8,128)(2,1)S(1)}, bf16[2,64,128]{2,1,0:T(8,128)(2,1)S(1)}, u32[]{:S(2)}, u32[]{:S(2)}) collective-permute-start(bf16[2,64,128]{2,1,0:T(8,128)(2,1)S(1)} %get-tuple-element.50), channel_id=1, source_target_pairs={{0,96},{32,64},{64,32},{96,0},{128,224},{160,192},{192,160},{224,1... | collective-permute-start | bytes 98312 | tf_op jit(solution)/shard_map/ppermute | solution.py:468
  30.7 1.6 %collective-permute-start.7 = (bf16[2,64,512]{2,1,0:T(8,128)(2,1)S(1)}, bf16[2,64,512]{2,1,0:T(8,128)(2,1)S(1)}, u32[]{:S(2)}, u32[]{:S(2)}) collective-permute-start(bf16[2,64,512]{2,1,0:T(8,128)(2,1)S(1)} %get-tuple-element.48), channel_id=1, source_target_pairs={{0,96},{32,64},{64,32},{96,0},{128,224},{160,192},{192,160},{224,1... | collective-permute-start | bytes 393224 | tf_op jit(solution)/shard_map/ppermute | solution.py:468
  32.3 1.4 %collective-permute-done.9.far_ref = bf16[2,64,128]{2,1,0:T(8,128)(2,1)S(1)} collective-permute-done((bf16[2,64,128]{2,1,0:T(8,128)(2,1)S(1)}, bf16[2,64,128]{2,1,0:T(8,128)(2,1)S(1)}, u32[]{:S(2)}, u32[]{:S(2)}) %collective-permute-start.9) | collective-permute-done | bytes 32800 | tf_op jit(solution)/shard_map/ppermute | solution.py:468
  33.7 1.5 %collective-permute-start.10 = (bf16[2,64,128]{2,1,0:T(8,128)(2,1)S(1)}, bf16[2,64,128]{2,1,0:T(8,128)(2,1)S(1)}, u32[]{:S(2)}, u32[]{:S(2)}) collective-permute-start(bf16[2,64,128]{2,1,0:T(8,128)(2,1)S(1)} %collective-permute-done.9.far_ref), channel_id=1, source_target_pairs={{0,1},{1,0},{2,3},{3,2},{4,5},{5,4},{6,7},{7,6},{8,9},{9,8},{10,11... | collective-permute-start | bytes 98312 | tf_op jit(solution)/shard_map/ppermute | solution.py:456
  35.2 0.9 %collective-permute-done.10.far_mate_ref = bf16[2,64,128]{2,1,0:T(8,128)(2,1)S(1)} collective-permute-done((bf16[2,64,128]{2,1,0:T(8,128)(2,1)S(1)}, bf16[2,64,128]{2,1,0:T(8,128)(2,1)S(1)}, u32[]{:S(2)}, u32[]{:S(2)}) %collective-permute-start.10) | collective-permute-done | bytes 32800 | tf_op jit(solution)/shard_map/ppermute | solution.py:456
  36.1 0.0 collective-permute-done.8.mate_ref
  36.1 2.4 %top_solve.1 = (f32[2,64,128]{2,1,0:T(8,128)S(1)}, f32[2,64,512]{2,1,0:T(8,128)S(1)}) custom-call(f32[2,64,640]{2,1,0:T(8,128)S(1)} %get-tuple-element.49.own_ref, f32[2,64,640]{2,1,0:T(8,128)S(1)} %collective-permute-done.8.mate_ref, bf16[2,64,128]{2,1,0:T(8,128)(2,1)S(1)} %collective-permute-done.9.far_ref, ...), custom_call_target="tpu_custom_call" | custom-call | flops 880000000 | tf_op jit(solution)/shard_map/top_solve/pallas_call | solution.py:444
  38.5 0.0 collective-permute-done.7.far_ref
  38.5 0.4 %collective-permute-start.11 = (bf16[2,64,512]{2,1,0:T(8,128)(2,1)S(1)}, bf16[2,64,512]{2,1,0:T(8,128)(2,1)S(1)}, u32[]{:S(2)}, u32[]{:S(2)}) collective-permute-start(bf16[2,64,512]{2,1,0:T(8,128)(2,1)S(1)} %collective-permute-done.7.far_ref), channel_id=1, source_target_pairs={{0,1},{1,0},{2,3},{3,2},{4,5},{5,4},{6,7},{7,6},{8,9},{9,8},{10,11... | collective-permute-start | bytes 393224 | tf_op jit(solution)/shard_map/ppermute | solution.py:456
  38.9 1.0 %collective-permute-done.11.far_mate_ref = bf16[2,64,512]{2,1,0:T(8,128)(2,1)S(1)} collective-permute-done((bf16[2,64,512]{2,1,0:T(8,128)(2,1)S(1)}, bf16[2,64,512]{2,1,0:T(8,128)(2,1)S(1)}, u32[]{:S(2)}, u32[]{:S(2)}) %collective-permute-start.11) | collective-permute-done | bytes 131104 | tf_op jit(solution)/shard_map/ppermute | solution.py:456
  39.9 1.0 %merge_top.1 = (f32[2,64,768]{2,1,0:T(8,128)}, f32[2,64,128]{2,1,0:T(8,128)}) custom-call(f32[2,64,128]{2,1,0:T(8,128)S(1)} %get-tuple-element.53.carried_ref, f32[2,64,512]{2,1,0:T(8,128)S(1)} %get-tuple-element.54.mine_ref, bf16[2,64,512]{2,1,0:T(8,128)(2,1)S(1)} %collective-permute-done.7.far_ref, bf16[2,64,512]{2,1,0:T(8,128)(2,1)S(1)} %collective-permute-done.11.far_mate_ref), custom_call_target="tpu_custom_call" | custom-call | flops 1100000000 | tf_op jit(solution)/shard_map/merge_top/pallas_call | solution.py:444
Async XLA Ops:
  0.6 11.2 %copy-start = (bf16[64,64,2,128]{3,2,1,0:T(2,128)(2,1)S(1)}, bf16[64,64,2,128]{3,2,1,0:T(2,128)(2,1)}, u32[]{:S(2)}) copy-start(bf16[64,64,2,128]{3,2,1,0:T(2,128)(2,1)} %guess_ref.1) | copy-start | bytes 6291460
  0.6 11.2 %copy-start.2 = (f32[64,64]{1,0:T(8,128)S(1)}, f32[64,64]{1,0:T(8,128)}, u32[]{:S(2)}) copy-start(f32[64,64]{1,0:T(8,128)} %coef_rows.1) | copy-start | bytes 49156
  0.7 11.2 %copy-start.1 = (bf16[64,64,2,128]{3,2,1,0:T(2,128)(2,1)S(1)}, bf16[64,64,2,128]{3,2,1,0:T(2,128)(2,1)}, u32[]{:S(2)}) copy-start(bf16[64,64,2,128]{3,2,1,0:T(2,128)(2,1)} %param.5) | copy-start | bytes 6291460
  0.7 13.8 %copy-start.3 = (bf16[1,1,2,256,4096]{4,3,2,1,0:T(8,128)(2,1)S(1)}, bf16[1,1,2,256,4096]{4,3,2,1,0:T(8,128)(2,1)}, u32[]{:S(2)}) copy-start(bf16[1,1,2,256,4096]{4,3,2,1,0:T(8,128)(2,1)} %param.9) | copy-start | bytes 12582916
  2.2 12.3 %collective-permute-start.3 = (bf16[896,128]{1,0:T(8,128)(2,1)S(1)}, bf16[896,128]{1,0:T(8,128)(2,1)S(1)}, u32[]{:S(2)}, u32[]{:S(2)}) collective-permute-start(bf16[896,128]{1,0:T(8,128)(2,1)S(1)} %get-tuple-element.34), channel_id=1, source_target_pairs={{0,32},{32,0},{64,96},{96,64},{128,160},{160,128},{192,224},{224,1... | collective-permute-start | bytes 688136 | tf_op jit(solution)/shard_map/ppermute | solution.py:456
  4.7 9.8 %collective-permute-start.1 = (bf16[128,128]{1,0:T(8,128)(2,1)S(1)}, bf16[128,128]{1,0:T(8,128)(2,1)S(1)}, u32[]{:S(2)}, u32[]{:S(2)}) collective-permute-start(bf16[128,128]{1,0:T(8,128)(2,1)S(1)} %bitcast.15), channel_id=1, source_target_pairs={{32,64},{64,32},{96,128},{128,96},{160,192},{192,160},{224,0},{0,2... | collective-permute-start | bytes 98312 | tf_op jit(solution)/shard_map/ppermute | solution.py:464
  9.4 5.1 %collective-permute-start = (bf16[128,128]{1,0:T(8,128)(2,1)S(1)}, bf16[128,128]{1,0:T(8,128)(2,1)S(1)}, u32[]{:S(2)}, u32[]{:S(2)}) collective-permute-start(bf16[128,128]{1,0:T(8,128)(2,1)S(1)} %bitcast.14), channel_id=1, source_target_pairs={{0,1},{1,0},{2,3},{3,2},{4,5},{5,4},{6,7},{7,6},{8,9},{9,8},{10,11... | collective-permute-start | bytes 98312 | tf_op jit(solution)/shard_map/ppermute | solution.py:456
  10.6 3.9 %collective-permute-start.2 = (bf16[128,128]{1,0:T(8,128)(2,1)S(1)}, bf16[128,128]{1,0:T(8,128)(2,1)S(1)}, u32[]{:S(2)}, u32[]{:S(2)}) collective-permute-start(bf16[128,128]{1,0:T(8,128)(2,1)S(1)} %bitcast.13), channel_id=1, source_target_pairs={{1,2},{2,1},{3,4},{4,3},{5,6},{6,5},{7,8},{8,7},{9,10},{10,9},{11,... | collective-permute-start | bytes 98312 | tf_op jit(solution)/shard_map/ppermute | solution.py:464
  16.5 7.0 %collective-permute-start.4 = (bf16[2,192,128]{2,1,0:T(8,128)(2,1)S(1)}, bf16[2,192,128]{2,1,0:T(8,128)(2,1)S(1)}, u32[]{:S(2)}, u32[]{:S(2)}) collective-permute-start(bf16[2,192,128]{2,1,0:T(8,128)(2,1)S(1)} %get-tuple-element.37), channel_id=1, source_target_pairs={{0,32},{32,0},{64,96},{96,64},{128,160},{160,128},{192,224},{224,1... | collective-permute-start | bytes 294920 | tf_op jit(solution)/shard_map/ppermute | solution.py:456
  19.3 6.5 %collective-permute-start.6 = (f32[2,128,384]{2,1,0:T(8,128)S(1)}, f32[2,128,384]{2,1,0:T(8,128)S(1)}, u32[]{:S(2)}, u32[]{:S(2)}) collective-permute-start(f32[2,128,384]{2,1,0:T(8,128)S(1)} %get-tuple-element.43.own_ref), channel_id=1, source_target_pairs={{0,1},{1,0},{2,3},{3,2},{4,5},{5,4},{6,7},{7,6},{8,9},{9,8},{10,11... | collective-permute-start | bytes 1179656 | tf_op jit(solution)/shard_map/ppermute | solution.py:456
  23.9 4.6 %collective-permute-start.5 = (f32[2,128,128]{2,1,0:T(8,128)S(1)}, f32[2,128,128]{2,1,0:T(8,128)S(1)}, u32[]{:S(2)}, u32[]{:S(2)}) collective-permute-start(f32[2,128,128]{2,1,0:T(8,128)S(1)} %get-tuple-element.41.own_ref), channel_id=1, source_target_pairs={{0,1},{1,0},{2,3},{3,2},{4,5},{5,4},{6,7},{7,6},{8,9},{9,8},{10,11... | collective-permute-start | bytes 393224 | tf_op jit(solution)/shard_map/ppermute | solution.py:456
  28.9 7.2 %collective-permute-start.8 = (f32[2,64,640]{2,1,0:T(8,128)S(1)}, f32[2,64,640]{2,1,0:T(8,128)S(1)}, u32[]{:S(2)}, u32[]{:S(2)}) collective-permute-start(f32[2,64,640]{2,1,0:T(8,128)S(1)} %get-tuple-element.49.own_ref), channel_id=1, source_target_pairs={{0,1},{1,0},{2,3},{3,2},{4,5},{5,4},{6,7},{7,6},{8,9},{9,8},{10,11... | collective-permute-start | bytes 983048 | tf_op jit(solution)/shard_map/ppermute | solution.py:456
  29.0 4.7 %collective-permute-start.9 = (bf16[2,64,128]{2,1,0:T(8,128)(2,1)S(1)}, bf16[2,64,128]{2,1,0:T(8,128)(2,1)S(1)}, u32[]{:S(2)}, u32[]{:S(2)}) collective-permute-start(bf16[2,64,128]{2,1,0:T(8,128)(2,1)S(1)} %get-tuple-element.50), channel_id=1, source_target_pairs={{0,96},{32,64},{64,32},{96,0},{128,224},{160,192},{192,160},{224,1... | collective-permute-start | bytes 98312 | tf_op jit(solution)/shard_map/ppermute | solution.py:468
  30.7 7.8 %collective-permute-start.7 = (bf16[2,64,512]{2,1,0:T(8,128)(2,1)S(1)}, bf16[2,64,512]{2,1,0:T(8,128)(2,1)S(1)}, u32[]{:S(2)}, u32[]{:S(2)}) collective-permute-start(bf16[2,64,512]{2,1,0:T(8,128)(2,1)S(1)} %get-tuple-element.48), channel_id=1, source_target_pairs={{0,96},{32,64},{64,32},{96,0},{128,224},{160,192},{192,160},{224,1... | collective-permute-start | bytes 393224 | tf_op jit(solution)/shard_map/ppermute | solution.py:468
  33.7 2.4 %collective-permute-start.10 = (bf16[2,64,128]{2,1,0:T(8,128)(2,1)S(1)}, bf16[2,64,128]{2,1,0:T(8,128)(2,1)S(1)}, u32[]{:S(2)}, u32[]{:S(2)}) collective-permute-start(bf16[2,64,128]{2,1,0:T(8,128)(2,1)S(1)} %collective-permute-done.9.far_ref), channel_id=1, source_target_pairs={{0,1},{1,0},{2,3},{3,2},{4,5},{5,4},{6,7},{7,6},{8,9},{9,8},{10,11... | collective-permute-start | bytes 98312 | tf_op jit(solution)/shard_map/ppermute | solution.py:456
  38.5 1.4 %collective-permute-start.11 = (bf16[2,64,512]{2,1,0:T(8,128)(2,1)S(1)}, bf16[2,64,512]{2,1,0:T(8,128)(2,1)S(1)}, u32[]{:S(2)}, u32[]{:S(2)}) collective-permute-start(bf16[2,64,512]{2,1,0:T(8,128)(2,1)S(1)} %collective-permute-done.7.far_ref), channel_id=1, source_target_pairs={{0,1},{1,0},{2,3},{3,2},{4,5},{5,4},{6,7},{7,6},{8,9},{9,8},{10,11... | collective-permute-start | bytes 393224 | tf_op jit(solution)/shard_map/ppermute | solution.py:456
